TPU v7x, 128 devices: a whole 4x4x4 slice. The times are simulated.
128 devices in a mesh: pipe: 2 (over z_lo), ctx: 32 (over y, z_hi, x), dp: 2 (over core).
Axes of the slice: x: 4, y: 4, z: 4 (z_hi: 2, z_lo: 2; z = z_hi * 2 + z_lo), core: 2. Of those that a mesh axis runs over, the one named last changes fastest.
Arguments:
- ahead_hidden: bfloat16 [2, 2, 4096, 16384], P('pipe', 'dp', 'ctx'), may hold values from -400 to 400
- ahead_queries: bfloat16 [2, 2, 4096, 2048], P('pipe', 'dp', 'ctx'), may hold values from -10 to 10
- behind_hidden: bfloat16 [2, 2, 4096, 16384], P('pipe', 'dp', 'ctx'), may hold values from -400 to 400
- behind_queries: bfloat16 [2, 2, 4096, 2048], P('pipe', 'dp', 'ctx'), may hold values from -10 to 10
- behind_cotangent: bfloat16 [2, 2, 4096, 2048], P('pipe', 'dp', 'ctx'), may hold values from -6 to 6
- keyval_weight: bfloat16 [2, 16384, 256], P('pipe', ('ctx', 'dp')), may hold values from -0.046875 to 0.046875
- norm_gain: bfloat16 [2, 16384], P('pipe'), may hold values from 0.25 to 1.75
- pair_of_rank: int32 [32], replicated, may hold values from 0 to 31, each once
Outputs:
- attention_out: bfloat16 [2, 2, 4096, 2048], P('pipe', 'dp', 'ctx')
- query_grad: bfloat16 [2, 2, 4096, 2048], P('pipe', 'dp', 'ctx')
- stream_grad: bfloat16 [2, 2, 4096, 16384], P('pipe', 'dp', 'ctx')
- keyval_grad: float32 [2, 16384, 256], P('pipe', ('ctx', 'dp'))
Inputs may be any that keep to these rules, and one draw needn't show every extreme that they name: Rank r holds the blocks pair_of_rank[r] and 63 - pair_of_rank[r] of the sequence's 2 * 32 blocks of 64 tokens; every pair is held once.
All inputs are finite; a program needn't handle non-finite values.
Results may differ from a plain program's by a relative error of at most 0.014.
Values may be sent and summed in bfloat16 or wider, within the bound.
A program may use at most 192 MiB of HBM per device.

v0:
```python
import jax
import jax.numpy as jnp
from jax import lax
from jax.sharding import PartitionSpec as P

DH = 128
HQ = 16


norm_eps = 1e-05


def shifted(x, axis, by):
    count = lax.axis_size(axis)
    pairs = [(i, i + by) for i in range(count) if 0 <= i + by < count]
    return lax.ppermute(x, axis, pairs)


def normalize(hidden, gain_row):
    hidden_wide = hidden.astype(jnp.float32)
    inverse = lax.rsqrt(jnp.mean(hidden_wide * hidden_wide, axis=-1, keepdims=True) + norm_eps)
    normed = (hidden_wide * inverse * gain_row.astype(jnp.float32)).astype(jnp.bfloat16)
    return (hidden_wide, inverse, normed)


def pair_lookup(pair_table, owners):
    ranks_all = jnp.arange(pair_table.shape[0], dtype=jnp.int32)
    matched = owners[:, None] == ranks_all[None, :]
    return jnp.sum(jnp.where(matched, pair_table[None, :], 0), axis=1)


def row_positions(pair_table, first_row, row_count, tok_rows):
    rows_all = first_row + jnp.arange(row_count, dtype=jnp.int32)
    owners = rows_all // tok_rows
    within = rows_all % tok_rows
    half_rows = tok_rows // 2
    paired = pair_lookup(pair_table, owners)
    slab_index = jnp.where(within < half_rows, paired, 2 * pair_table.shape[0] - 1 - paired)
    return slab_index * half_rows + within % half_rows


def masked_weights(query_rows, row_position, key_rows, key_position):
    scores = lax.dot_general(
        query_rows, key_rows, (((1,), (1,)), ((), ())), preferred_element_type=jnp.float32
    ) * DH ** (-0.5)
    visible = key_position[None, :] <= row_position[:, None]
    return jnp.where(visible, jnp.exp(scores), 0.0)


def local_rows(queries, pair_table, ctx_index):
    tok_rows = queries.shape[0]
    query_rows = queries.reshape(tok_rows * HQ, DH)
    own_position = row_positions(pair_table, ctx_index * tok_rows, tok_rows, tok_rows)
    return (query_rows, jnp.repeat(own_position, HQ))


def forward_layer(hidden, queries, gain_row, weight, pair_table, ctx_index):
    tok_rows = hidden.shape[0]
    hidden_wide, inverse, normed = normalize(hidden, gain_row)
    keyval = jnp.dot(normed, weight, preferred_element_type=jnp.float32).astype(jnp.bfloat16)
    query_rows, row_position = local_rows(queries, pair_table, ctx_index)
    shard_rows = lax.all_gather(keyval, "ctx", axis=0, tiled=True)
    key_position = row_positions(pair_table, jnp.int32(0), shard_rows.shape[0], tok_rows)
    weights = masked_weights(query_rows, row_position, shard_rows[:, :DH], key_position)
    summed = jnp.dot(
        weights.astype(jnp.bfloat16), shard_rows[:, DH:], preferred_element_type=jnp.float32
    )
    row_total, summed = (jnp.sum(weights, axis=1), summed)
    return (summed / row_total[:, None]).astype(jnp.bfloat16).reshape(tok_rows, HQ * DH)


def backward_layer(hidden, queries, cotangent, gain_row, weight, pair_table, ctx_index):
    tok_rows = hidden.shape[0]
    hidden_wide, inverse, normed = normalize(hidden, gain_row)
    keyval = jnp.dot(normed, weight, preferred_element_type=jnp.float32).astype(jnp.bfloat16)
    gathered = lax.all_gather(keyval, "ctx", axis=0, tiled=True)
    seq_rows = gathered.shape[0]
    ctx_count = seq_rows // tok_rows
    block_shards = min(ctx_count, max(1, 1024 // tok_rows))
    block_rows = block_shards * tok_rows
    block_count = seq_rows // block_rows
    key_blocks = gathered.reshape(block_count, block_rows, 2 * DH)
    block_starts = jnp.arange(block_count, dtype=jnp.int32) * block_rows
    query_rows, row_position = local_rows(queries, pair_table, ctx_index)
    grad_out_rows = cotangent.reshape(tok_rows * HQ, DH)

    def stats_step(totals, inputs):
        block_keys, first_row = inputs
        key_position = row_positions(pair_table, first_row, block_rows, tok_rows)
        weights = masked_weights(query_rows, row_position, block_keys[:, :DH], key_position)
        summed = jnp.dot(
            weights.astype(jnp.bfloat16), block_keys[:, DH:], preferred_element_type=jnp.float32
        )
        return ((totals[0] + jnp.sum(weights, axis=1), totals[1] + summed), None)

    start_totals = (
        jnp.zeros((tok_rows * HQ,), jnp.float32),
        jnp.zeros((tok_rows * HQ, DH), jnp.float32),
    )
    (row_total, summed), unused = lax.scan(stats_step, start_totals, (key_blocks, block_starts))
    outputs = summed / row_total[:, None]
    row_delta = jnp.sum(grad_out_rows.astype(jnp.float32) * outputs, axis=1)
    head_scale = DH ** (-0.5)

    def grad_step(grad_rows, inputs):
        block_keys, first_row = inputs
        key_position = row_positions(pair_table, first_row, block_rows, tok_rows)
        prob_rows = (
            masked_weights(query_rows, row_position, block_keys[:, :DH], key_position)
            / row_total[:, None]
        )
        grad_values = lax.dot_general(
            prob_rows.astype(jnp.bfloat16),
            grad_out_rows,
            (((0,), (0,)), ((), ())),
            preferred_element_type=jnp.float32,
        )
        grad_probs = lax.dot_general(
            grad_out_rows,
            block_keys[:, DH:],
            (((1,), (1,)), ((), ())),
            preferred_element_type=jnp.float32,
        )
        grad_scores = (prob_rows * (grad_probs - row_delta[:, None])).astype(jnp.bfloat16)
        grad_rows = grad_rows + jnp.dot(
            grad_scores, block_keys[:, :DH], preferred_element_type=jnp.float32
        )
        grad_keys = (
            lax.dot_general(
                grad_scores,
                query_rows,
                (((0,), (0,)), ((), ())),
                preferred_element_type=jnp.float32,
            )
            * head_scale
        )
        return (grad_rows, jnp.concatenate([grad_keys, grad_values], axis=1))

    grad_rows, key_terms = lax.scan(
        grad_step, jnp.zeros((tok_rows * HQ, DH), jnp.float32), (key_blocks, block_starts)
    )
    key_terms = key_terms.reshape(seq_rows, 2 * DH)
    key_grads = lax.psum_scatter(key_terms, "ctx", scatter_dimension=0, tiled=True).astype(
        jnp.bfloat16
    )
    grad_normed = lax.dot_general(
        key_grads, weight, (((1,), (1,)), ((), ())), preferred_element_type=jnp.float32
    )
    scaled = gain_row.astype(jnp.float32) * grad_normed
    inner_sum = jnp.mean(hidden_wide * scaled, axis=-1, keepdims=True)
    stream_term = inverse * scaled - hidden_wide * (inverse * inverse * inverse) * inner_sum
    query_grad = (grad_rows * head_scale).astype(jnp.bfloat16).reshape(tok_rows, HQ * DH)
    return (query_grad, stream_term, normed, key_grads)


def body(
    ahead_hidden,
    ahead_queries,
    behind_hidden,
    behind_queries,
    behind_cotangent,
    keyval_weight,
    norm_gain,
    pair_of_rank,
):
    ctx_index = lax.axis_index("ctx")
    gain_row = norm_gain[0]
    weight = lax.all_gather(keyval_weight[0], ("ctx", "dp"), axis=0, tiled=True)
    attention_out = forward_layer(
        ahead_hidden[0, 0], ahead_queries[0, 0], gain_row, weight, pair_of_rank, ctx_index
    )
    backward_parts = backward_layer(
        behind_hidden[0, 0],
        behind_queries[0, 0],
        behind_cotangent[0, 0],
        gain_row,
        weight,
        pair_of_rank,
        ctx_index,
    )
    query_grad, stream_term, normed, key_grads = backward_parts
    own_term = stream_term.astype(jnp.bfloat16)
    later_term = shifted(own_term, "pipe", -1)
    stream_grad = (stream_term + later_term.astype(jnp.float32)).astype(jnp.bfloat16)
    partial_grad = lax.dot_general(
        normed, key_grads, (((0,), (0,)), ((), ())), preferred_element_type=jnp.float32
    )
    weight_grad = lax.psum_scatter(partial_grad, ("ctx", "dp"), scatter_dimension=0, tiled=True)
    return (
        attention_out[None, None],
        query_grad[None, None],
        stream_grad[None, None],
        weight_grad[None],
    )


def solution(mesh):
    in_specs = (
        P("pipe", "dp", "ctx", None),
        P("pipe", "dp", "ctx", None),
        P("pipe", "dp", "ctx", None),
        P("pipe", "dp", "ctx", None),
        P("pipe", "dp", "ctx", None),
        P("pipe", ("ctx", "dp"), None),
        P("pipe", None),
        P(),
    )
    out_specs = (
        P("pipe", "dp", "ctx", None),
        P("pipe", "dp", "ctx", None),
        P("pipe", "dp", "ctx", None),
        P("pipe", ("ctx", "dp"), None),
    )
    return jax.shard_map(body, mesh=mesh, in_specs=in_specs, out_specs=out_specs, check_vma=False)
```

profile of v0, /device:TPU:32, one launch (start us, length us, event | category | flops | bytes accessed | tf_op | source)
XLA Modules:
  0.0 895.0 jit_solution(3062719673052233858)
XLA Ops:
  8.9 3.1 fusion.48
  12.6 83.5 %all-gather.9.cloned.1.call-done = bf16[1,16384,256]{2,1,0:T(8,128)(2,1)} async-done(((bf16[1,256,256]{2,1,0:T(8,128)(2,1)}), bf16[1,16384,256]{2,1,0:T(8,128)(2,1)}) %all-gather.9.cloned.1.call-update) | async-done | bytes 8388624 | tf_op jit(solution)/shard_map/all_gather | solution.py:168
  96.1 6.7 fusion.79
  103.5 68.3 %all-gather.7.cloned.1.call-done = bf16[4096,256]{1,0:T(8,128)(2,1)} async-done(((bf16[128,256]{1,0:T(8,128)(2,1)}), bf16[4096,256]{1,0:T(8,128)(2,1)}) %all-gather.7.cloned.1.call-update) | async-done | bytes 2097168 | tf_op jit(solution)/shard_map/all_gather | solution.py:76
  171.8 30.3 %while.32 = (s32[]{:T(128)}, f32[2048]{0:T(1024)S(1)}, f32[2048,128]{1,0:T(8,128)S(1)}, s32[4]{0:T(128)S(1)}, s32[32]{0:T(128)S(1)}, /*index=5*/bf16[4,1024,256]...) while((s32[]{:T(128)}, f32[2048]{0:T(1024)S(1)}, ...), condition=%wide.region_8.9_spmd.clone, body=%wide.region_5.8_spmd.clone.sunk | while | flops 1091187712 | bytes 21074704 | solution.py:100
  174.0 1.1 dynamic-slice_bitcast_fusion.4
  175.1 2.0 fusion.134
  177.1 2.3 fusion.135
  182.7 2.0 fusion.134
  184.7 2.3 fusion.135
  190.2 2.0 fusion.134
  192.2 2.3 fusion.135
  197.8 2.0 fusion.134
  199.8 2.3 fusion.135
  202.7 57.1 %while.33 = (s32[]{:T(128)}, f32[2048,128]{1,0:T(8,128)}, f32[4,1024,256]{2,1,0:T(8,128)}, s32[4]{0:T(128)S(1)}, s32[32]{0:T(128)S(1)}, /*index=5*/bf16[4,1024,2...) while((s32[]{:T(128)}, f32[2048,128]{1,0:T(8,128)}, ...), condition=%wide.region_12.13_spmd.clone, body=%wide.region_10.12_spmd.clone.sunk | while | flops 2702191616 | bytes 51192616 | solution.py:139
  206.0 2.0 fusion.147
  208.0 1.5 fusion.149
  209.5 1.3 fusion.148
  210.8 2.3 convolution_add_fusion.2
  213.1 1.5 convolution_multiply_fusion.3
  219.3 2.0 fusion.147
  221.3 1.5 fusion.149
  222.9 1.3 fusion.148
  224.1 3.5 convolution_add_fusion.2
  227.7 1.5 convolution_multiply_fusion.3
  233.9 2.0 fusion.147
  235.9 1.5 fusion.149
  237.4 1.3 fusion.148
  238.7 3.5 convolution_add_fusion.2
  242.2 1.5 convolution_multiply_fusion.3
  248.5 2.0 fusion.147
  250.5 1.5 fusion.149
  252.0 1.3 fusion.148
  253.3 3.5 convolution_add_fusion.2
  256.8 1.5 convolution_multiply_fusion.3
  260.1 3.1 fusion.45
  263.2 6.7 fusion.74
  270.0 179.3 %reduce-scatter.3.cloned.1.call-done = f32[128,256]{1,0:T(8,128)} async-done(((f32[4096,256]{1,0:T(8,128)}), f32[128,256]{1,0:T(8,128)}) %reduce-scatter.3.cloned.1.call-update) | async-done | bytes 131088 | tf_op jit(solution)/shard_map/reduce_scatter | solution.py:143
  449.3 10.4 %fusion.71 = f32[16384,256]{1,0:T(8,128)} fusion(bf16[1,1,128,16384]{3,2,1,0:T(8,128)(2,1)} %param.14, f32[128]{0:T(128)S(1)} %copy-done.10, f32[16384]{0:T(1024)S(1)} %bitcast.125, f32[128,256]{1,0:T(8,128)} %reduce-scatter.3.cloned.1.call-done), kind=kOutput, calls=%fused_computation.105 | convolution fusion | flops 1082163200 | bytes 21168640 | tf_op jit(solution)/shard_map/dot_general | solution.py:185
  461.2 7.7 fusion.53
  468.9 4.7 fusion.59
  473.6 5.1 collective-permute-start
  478.8 1.3 multiply_convert_fusion
  481.1 48.3 %all-gather.5.cloned.1.call-done = bf16[4096,256]{1,0:T(8,128)(2,1)} async-done(((bf16[128,256]{1,0:T(8,128)(2,1)}), bf16[4096,256]{1,0:T(8,128)(2,1)}) %all-gather.5.cloned.1.call-update) | async-done | bytes 2097168 | tf_op jit(solution)/shard_map/all_gather | solution.py:62
  529.4 15.6 %fusion.40 = (f32[2048]{0:T(1024)S(1)}, f32[4096,2048]{1,0:T(8,128)}) fusion(s32[2048]{0:T(1024)S(1)} %le.80, s32[4096]{0:T(1024)S(1)} %fusion.91, bf16[2048,128]{1,0:T(8,128)(2,1)S(1)} %reshape_squeeze.9, bf16[4096,256]{1,0:T(8,128)(2,1)} %all-gather.5.cloned.1.call-done), kind=kOutput, calls=%fused_computation.72 | convolution fusion | flops 2181036032 | bytes 35160064 | tf_op jit(solution)/shard_map/dot_general | solution.py:43
  545.0 13.8 %fusion.68 = bf16[2048,128]{1,0:T(8,128)(2,1)S(1)} fusion(f32[4096,2048]{1,0:T(8,128)} %get-tuple-element.434, s32[2048]{0:T(1024)S(1)} %le.80, s32[4096]{0:T(1024)S(1)} %fusion.91, bf16[4096,256]{1,0:T(8,128)(2,1)S(1)} %copy-done.12, f32[2048]{0:T(1024)S(1)} %get-tuple-element.433), kind=kOutput, calls=%fused_computation.104 | convolution fusion | flops 2181562368 | bytes 35160064 | tf_op jit(solution)/shard_map/dot_general | solution.py:65
  560.7 9.0 %fusion.60 = bf16[1,1,128,16384]{3,2,1,0:T(8,128)(2,1)} fusion(bf16[128,16384]{1,0:T(8,128)(2,1)} %collective-permute-done, f32[128,16384]{1,0:T(8,128)} %copy-done.1, bf16[1,1,128,16384]{3,2,1,0:T(8,128)(2,1)} %param.14, f32[128]{0:T(128)S(1)} %broadcast_multiply_fusion, f32[128]{0:T(128)S(1)} %copy-done.11, f32[128]{0:T(128)S(1)} %copy-done.10), kind=kLoop, calls=%fused_computation.99 | loop fusion | flops 16777216 | bytes 20973056 | tf_op jit(solution)/shard_map/broadcast_in_dim | solution.py:192
  569.7 318.7 %reduce-scatter.5.cloned.1.call-done = f32[256,256]{1,0:T(8,128)} async-done(((f32[16384,256]{1,0:T(8,128)}), f32[256,256]{1,0:T(8,128)}) %reduce-scatter.5.cloned.1.call-update) | async-done | bytes 262160 | tf_op jit(solution)/shard_map/reduce_scatter | solution.py:188
  (131 shorter events, 39.0 us)
Async XLA Ops:
  7.2 88.9 %all-gather.9.cloned.1.call-start = ((), (), s32[]{:S(2)}) async-start(), calls=%async_computation.6 | async-start | bytes 8519680 | tf_op jit(solution)/shard_map/all_gather | solution.py:168
  7.9 163.9 %all-gather.7.cloned.1.call-start = ((), (), s32[]{:S(2)}) async-start(), calls=%async_computation.3 | async-start | bytes 2162688 | tf_op jit(solution)/shard_map/all_gather | solution.py:76
  8.9 93.9 %copy-start.2 = (f32[1,16384]{1,0:T(1,128)}, f32[1,16384]{1,0:T(1,128)S(1)}, u32[]{:S(2)}) copy-start(f32[1,16384]{1,0:T(1,128)S(1)} %mul.205) | copy-start | bytes 196612
  12.6 90.2 %copy-start.9 = (f32[128]{0:T(128)}, f32[128]{0:T(128)S(1)}, u32[]{:S(2)}) copy-start(f32[128]{0:T(128)S(1)} %get-tuple-element.432) | copy-start | bytes 1540
  96.1 6.8 copy-start.5
  96.1 7.1 copy-start.6
  96.1 7.3 copy-start.8
  102.8 346.6 %reduce-scatter.3.cloned.1.call-start = ((), (), s32[]{:S(2)}) async-start(), calls=%async_computation.4 | async-start | bytes 4325376 | tf_op jit(solution)/shard_map/reduce_scatter | solution.py:143
  259.8 3.4 copy-start.3
  259.8 269.6 %all-gather.5.cloned.1.call-start = ((), (), s32[]{:S(2)}) async-start(), calls=%async_computation.2 | async-start | bytes 2162688 | tf_op jit(solution)/shard_map/all_gather | solution.py:62
  263.2 186.1 %copy-start.10 = (f32[128]{0:T(128)S(1)}, f32[128]{0:T(128)}, u32[]{:S(2)}) copy-start(f32[128]{0:T(128)} %copy-done.9) | copy-start | bytes 1540
  269.9 618.5 %reduce-scatter.5.cloned.1.call-start = ((), (), s32[]{:S(2)}) async-start(), calls=%async_computation.5 | async-start | bytes 17039360 | tf_op jit(solution)/shard_map/reduce_scatter | solution.py:188
  459.7 1.0 copy-start.7
  459.7 1.5 copy-start.4
  461.1 7.7 copy-start
  461.2 7.7 copy-start.11
  468.9 4.8 copy-start.1
  473.6 87.0 %collective-permute-start = (bf16[128,16384]{1,0:T(8,128)(2,1)}, bf16[128,16384]{1,0:T(8,128)(2,1)}, u32[]{:S(2)}, u32[]{:S(2)}) collective-permute-start(bf16[128,16384]{1,0:T(8,128)(2,1)} %fusion.59), channel_id=1, source_target_pairs={{64,0},{65,1},{66,2},{67,3},{68,4},{69,5},{70,6},{71,7},{72,8},{73... | collective-permute-start | bytes 12582920 | tf_op jit(solution)/shard_map/ppermute | solution.py:16
  529.4 15.6 %copy-start.12 = (bf16[4096,256]{1,0:T(8,128)(2,1)S(1)}, bf16[4096,256]{1,0:T(8,128)(2,1)}, u32[]{:S(2)}) copy-start(bf16[4096,256]{1,0:T(8,128)(2,1)} %all-gather.5.cloned.1.call-done) | copy-start | bytes 6291460
Sparse Core Ops, SparseCore 0:
  11.2 84.7 all-gather.8
  102.9 68.9 all-gather.6
  259.9 189.3 reduce-scatter.2
  452.8 76.5 all-gather.4
  532.2 356.1 reduce-scatter.4
where the time goes:
time: 897 us; the launch traced here: 895 us
  waiting for transfers between devices  700 us (78%)
  matrix products  116 us (13%)
  other arithmetic  35.3 us (4%)
  local copies, waits for them, and re-layouts  24 us (3%)
  between operations  14 us (2%)
    reduce_scatter x1, waiting for transfers between devices, body(): lax.psum_scatter(partial_grad, ('ctx', 'dp'), scatter_dimension=0, tiled=...  319 us
    reduce_scatter x1, waiting for transfers between devices, backward_layer(): lax.psum_scatter(key_terms, 'ctx', scatter_dimension=0, tiled=True)  179 us
    all_gather x1, waiting for transfers between devices, body(): weight = lax.all_gather(keyval_weight[0], ('ctx', 'dp'), axis=0, tiled=True)  83.5 us
    all_gather x1, waiting for transfers between devices, backward_layer(): gathered = lax.all_gather(keyval, 'ctx', axis=0, tiled=True)  68.3 us
    all_gather x1, waiting for transfers between devices, forward_layer(): shard_rows = lax.all_gather(keyval, 'ctx', axis=0, tiled=True)  48.3 us
    dot_general x9, matrix products, masked_weights(): lax.dot_general(query_rows, key_rows, (((1,), (1,)), ((), ())), preferred...  31.4 us
  transfers between devices with their start and end apart: 6, of which 6 were waited for; matrix products, arithmetic and copies ran while one was open for 9% of the time, Pallas kernels for 0%

commit v1 on v0

v1 whole, which is shorter than its diff:
```python
import jax
import jax.numpy as jnp
from jax import lax
from jax.experimental import pallas as pl
from jax.experimental.pallas import tpu as pltpu
from jax.sharding import PartitionSpec as P

D = 16384
DH = 128
HQ = 16
TOK = 128
KVW = 256
RANKS = 32
SEQ = RANKS * TOK
HALF = TOK // 2
CHUNK = 512
TILE = 256
NORM_EPS = 1e-05
SCALE = DH ** (-0.5)
EXP_SCALE = SCALE * 1.4426950408889634
F32 = jnp.float32
BF16 = jnp.bfloat16
MESH = pl.DeviceIdType.MESH
MIB = 1024 * 1024

ORDER = ((0, 0), (0, 1), (-1, 0), (1, 0), (-1, 1), (1, 1), (2, 0), (2, 1))


def rid(du, dv, zr):
    return ((dv % 4) * 4 + du % 4) * 2 + zr


class Place:
    def __init__(self):
        self.pipe = lax.axis_index("pipe")
        ctx = lax.axis_index("ctx")
        core = lax.axis_index("dp")
        y, z, x = ctx // 8, (ctx // 4) % 2, ctx % 4
        self.ctx, self.core, self.z = ctx, core, z
        self.u = x * (1 - core) + y * core
        self.v = y * (1 - core) + x * core
        self.su = 1 + 7 * core
        self.sv = 8 - 7 * core

    def slot(self, du, dv, zr):
        z = self.z if zr == 0 else 1 - self.z
        return ((self.u + du + 4) % 4) * self.su + ((self.v + dv + 4) % 4) * self.sv + z * 4

    def sibling_slot(self, du, dv, zr):
        z = self.z if zr == 0 else 1 - self.z
        return ((self.v + du + 4) % 4) * self.sv + ((self.u + dv + 4) % 4) * self.su + z * 4

    def device(self, du, dv, zr):
        return (self.pipe, self.slot(du, dv, zr), self.core)

    def sibling(self):
        return (self.pipe, self.ctx, 1 - self.core)

    def barrier(self):
        semaphore = pltpu.get_barrier_semaphore()
        partners = [
            self.device(0, 0, 1),
            self.device(1, 0, 0),
            self.device(-1, 0, 0),
            self.device(0, 1, 0),
            self.device(0, -1, 0),
            self.sibling(),
        ]
        for partner in partners:
            pl.semaphore_signal(semaphore, inc=1, device_id=partner, device_id_type=MESH)
        pl.semaphore_wait(semaphore, len(partners))


class Sender:
    def __init__(self, send_sems):
        self.send_sems = send_sems
        self.copies = []

    def push(self, src, dst, recv_sem, device):
        copy = pltpu.make_async_remote_copy(
            src_ref=src,
            dst_ref=dst,
            send_sem=self.send_sems.at[len(self.copies)],
            recv_sem=recv_sem,
            device_id=device,
            device_id_type=MESH,
        )
        copy.start()
        self.copies.append(copy)

    def landed(self, dst, recv_sem, device):
        pltpu.make_async_remote_copy(
            src_ref=dst,
            dst_ref=dst,
            send_sem=self.send_sems.at[0],
            recv_sem=recv_sem,
            device_id=device,
            device_id_type=MESH,
        ).wait_recv()

    def finish(self):
        for copy in self.copies:
            copy.wait_send()


def ring_gather(place, sender, at, recv, to_sibling, hook):
    z_mate = place.device(0, 0, 1)
    u_right, u_left = place.device(1, 0, 0), place.device(-1, 0, 0)
    v_right, v_left = place.device(0, 1, 0), place.device(0, -1, 0)

    def send(slot, seen, device):
        sender.push(at(slot), at(slot), recv.at[rid(*seen)], device)

    def wait(du, dv, zr):
        slot = place.slot(du, dv, zr)
        sender.landed(at(slot), recv.at[rid(du, dv, zr)], z_mate)
        return slot

    own = place.slot(0, 0, 0)
    send(own, (0, 0, 1), z_mate)
    send(own, (-1, 0, 0), u_right)
    send(own, (1, 0, 0), u_left)
    send(own, (0, -1, 0), v_right)
    send(own, (0, 1, 0), v_left)
    to_sibling(own, 0, 0, 0)
    hook(own)
    for du, zr in ORDER[1:]:
        slot = wait(du, 0, zr)
        if du == 0:
            send(slot, (-1, 0, 1), u_right)
            send(slot, (1, 0, 1), u_left)
        elif du == -1 and zr == 0:
            send(slot, (2, 0, 0), u_right)
        elif du == 1 and zr == 1:
            send(slot, (2, 0, 1), u_left)
        send(slot, (du, -1, zr), v_right)
        send(slot, (du, 1, zr), v_left)
        to_sibling(slot, du, 0, zr)
        hook(slot)
    for du, zr in ORDER:
        for dv in (-1, 1):
            slot = wait(du, dv, zr)
            if dv == -1 and zr == 0:
                send(slot, (du, 2, 0), v_right)
            elif dv == 1 and zr == 1:
                send(slot, (du, 2, 1), v_left)
            to_sibling(slot, du, dv, zr)
            hook(slot)
    for du, zr in ORDER:
        slot = wait(du, 2, zr)
        to_sibling(slot, du, 2, zr)
        hook(slot)


def ring_sum(place, sender, term, got, recv, make):
    z_mate = place.device(0, 0, 1)
    u_right, u_left = place.device(1, 0, 0), place.device(-1, 0, 0)
    v_right, v_left = place.device(0, 1, 0), place.device(0, -1, 0)

    def send(slot, index, device):
        sender.push(term(slot), got.at[index], recv.at[index], device)

    def wait(index):
        sender.landed(got.at[index], recv.at[index], z_mate)
        return got[index].astype(F32)

    def add(slot, *indices):
        total = term(slot)[...].astype(F32)
        for index in indices:
            total = total + wait(index)
        term(slot)[...] = total.astype(BF16)

    far = (2, -1, 1, 0)
    for k, du in enumerate(far):
        slot = place.slot(du, 2, 0)
        make(slot)
        send(slot, k, v_right)
        slot = place.slot(du, 2, 1)
        make(slot)
        send(slot, 4 + k, v_left)
    for k, du in enumerate(far):
        slot = place.slot(du, 1, 1)
        make(slot)
        send(slot, 8 + 2 * k + 1, v_right)
        slot = place.slot(du, -1, 0)
        make(slot)
        send(slot, 16 + 2 * k, v_left)
    for k, du in enumerate(far):
        slot = place.slot(du, 1, 0)
        make(slot)
        add(slot, k)
        send(slot, 8 + 2 * k, v_right)
        slot = place.slot(du, -1, 1)
        make(slot)
        add(slot, 4 + k)
        send(slot, 16 + 2 * k + 1, v_left)
    for du in far:
        for zr in (0, 1):
            make(place.slot(du, 0, zr))
    for k, du in enumerate(far):
        for zr in (1, 0):
            add(place.slot(du, 0, zr), 8 + 2 * k + zr, 16 + 2 * k + zr)
        if du == 2:
            send(place.slot(2, 0, 0), 24, u_right)
            send(place.slot(2, 0, 1), 25, u_left)
        elif du == -1:
            send(place.slot(-1, 0, 0), 28, u_left)
            add(place.slot(-1, 0, 1), 25)
            send(place.slot(-1, 0, 1), 29, u_left)
        elif du == 1:
            send(place.slot(1, 0, 1), 27, u_right)
            add(place.slot(1, 0, 0), 24)
            send(place.slot(1, 0, 0), 26, u_right)
    other = place.slot(0, 0, 1)
    add(other, 27, 29)
    send(other, 30, z_mate)
    total = term(place.slot(0, 0, 0))[...].astype(F32)
    for index in (26, 28, 30):
        total = total + wait(index)
    return total


def gather_kernel(
    gain_ref,
    ahead_ref,
    behind_ref,
    weight_ref,
    weight_out,
    keyval_out,
    pair_out,
    stat_out,
    hidden,
    normed,
    weights,
    keyvals,
    total,
    load_sems,
    send_sems,
    weight_recv,
    sibling_recv,
    keyval_recv,
    pair_recv,
):
    place = Place()
    sender = Sender(send_sems)
    core = place.core
    loads = [
        pltpu.make_async_copy(behind_ref, hidden.at[1], load_sems.at[0]),
        pltpu.make_async_copy(ahead_ref, hidden.at[0], load_sems.at[1]),
    ]
    own_load = pltpu.make_async_copy(weight_ref, weights.at[place.ctx, core], load_sems.at[2])
    own_load.start()
    for load in loads:
        load.start()
    place.barrier()
    own_load.wait()
    total[...] = jnp.zeros_like(total)
    inverses = {}

    def row_scale(batch):
        def step(j, squares):
            block = hidden[batch, :, pl.ds(pl.multiple_of(j * KVW, KVW), KVW)].astype(F32)
            block = block * block
            return squares + block[:, :DH] + block[:, DH:]

        squares = lax.fori_loop(0, D // KVW, step, jnp.zeros((TOK, DH), F32), unroll=4)
        mean = jnp.sum(squares, axis=1, keepdims=True) * (1.0 / D)
        inverses[batch] = lax.rsqrt(mean + NORM_EPS)

    def scale_rows(batch, part):
        inverse = inverses[batch]

        @pl.loop(part * 16, part * 16 + 16)
        def _(i):
            for k in range(2):
                columns = pl.ds(pl.multiple_of((2 * i + k) * KVW, KVW), KVW)
                block = hidden[batch, :, columns].astype(F32) * inverse * gain_ref[2 * i + k]
                normed[i, k, batch * TOK : (batch + 1) * TOK, :] = block.astype(BF16)

    def send_pair():
        sender.push(
            normed.at[:, 1 - core, pl.ds(TOK, TOK), :],
            pair_out.at[:, pl.ds(pl.multiple_of(core * TOK, TOK), TOK), :],
            pair_recv,
            place.sibling(),
        )
        own_pair.start()

    own_pair = pltpu.make_async_copy(
        normed.at[:, core, pl.ds(TOK, TOK), :],
        pair_out.at[:, pl.ds(pl.multiple_of(core * TOK, TOK), TOK), :],
        load_sems.at[3],
    )
    todo = [
        lambda: (loads[0].wait(), row_scale(1)),
        lambda: scale_rows(1, 0),
        lambda: scale_rows(1, 1),
        lambda: (send_pair(), loads[1].wait(), row_scale(0)),
        lambda: scale_rows(0, 0),
        lambda: scale_rows(0, 1),
    ]
    ready = []
    arrived = [0]
    sibling_order = [(du, 0, zr) for du, zr in ORDER]
    sibling_order += [(du, dv, zr) for du, zr in ORDER for dv in (-1, 1)]
    sibling_order += [(du, 2, zr) for du, zr in ORDER]
    taken = [0]

    def project(ctx, which):
        total[...] += jnp.dot(normed[ctx, which], weights[ctx, which], preferred_element_type=F32)

    def take_sibling():
        du, dv, zr = sibling_order[taken[0]]
        taken[0] += 1
        slot = place.sibling_slot(du, dv, zr)
        sender.landed(weights.at[slot, 1 - core], sibling_recv.at[rid(du, dv, zr)], place.sibling())
        project(slot, 1 - core)

    def on_weight(slot):
        ready.append(slot)
        arrived[0] += 1
        if todo:
            todo.pop(0)()
        else:
            while ready:
                project(ready.pop(0), core)
            for _ in range(2):
                if taken[0] + 2 < arrived[0]:
                    take_sibling()

    def to_sibling(slot, du, dv, zr):
        sender.push(
            weights.at[slot, core],
            weights.at[slot, core],
            sibling_recv.at[rid(du, dv, zr)],
            place.sibling(),
        )

    ring_gather(place, sender, lambda slot: weights.at[slot, core], weight_recv, to_sibling, on_weight)
    while taken[0] < len(sibling_order):
        take_sibling()
    weight_store = pltpu.make_async_copy(weights, weight_out, load_sems.at[2])
    weight_store.start()
    keyvals[place.ctx] = total[...].astype(BF16)
    ring_gather(
        place,
        sender,
        lambda slot: keyvals.at[slot],
        keyval_recv,
        lambda *unused: None,
        lambda unused: None,
    )
    keyval_store = pltpu.make_async_copy(keyvals, keyval_out, load_sems.at[0])
    keyval_store.start()
    stat_out[0] = jnp.broadcast_to(inverses[1], (TOK, KVW))
    stat_out[1] = total[TOK:, :]
    sender.landed(
        pair_out.at[:, pl.ds(pl.multiple_of((1 - core) * TOK, TOK), TOK), :], pair_recv, place.sibling()
    )
    own_pair.wait()
    weight_store.wait()
    keyval_store.wait()
    sender.finish()


def gather_call(gain, ahead, behind, weight):
    any_spec = pl.BlockSpec(memory_space=pl.ANY)
    vmem_spec = pl.BlockSpec(memory_space=pltpu.VMEM)
    return pl.pallas_call(
        gather_kernel,
        name="gather_project",
        out_shape=(
            jax.ShapeDtypeStruct((RANKS, 2, KVW, KVW), BF16),
            jax.ShapeDtypeStruct((RANKS, KVW, KVW), BF16),
            jax.ShapeDtypeStruct((RANKS, KVW, KVW), BF16),
            jax.ShapeDtypeStruct((2, TOK, KVW), F32),
        ),
        in_specs=[vmem_spec, any_spec, any_spec, any_spec],
        out_specs=(any_spec, any_spec, any_spec, vmem_spec),
        scratch_shapes=[
            pltpu.VMEM((2, TOK, D), BF16),
            pltpu.VMEM((RANKS, 2, KVW, KVW), BF16),
            pltpu.VMEM((RANKS, 2, KVW, KVW), BF16),
            pltpu.VMEM((RANKS, KVW, KVW), BF16),
            pltpu.VMEM((KVW, KVW), F32),
            pltpu.SemaphoreType.DMA((4,)),
            pltpu.SemaphoreType.DMA((128,)),
            pltpu.SemaphoreType.DMA((32,)),
            pltpu.SemaphoreType.DMA((32,)),
            pltpu.SemaphoreType.DMA((32,)),
            pltpu.SemaphoreType.DMA,
        ],
        compiler_params=pltpu.CompilerParams(
            collective_id=0, has_side_effects=True, vmem_limit_bytes=50 * MIB
        ),
        cost_estimate=pl.CostEstimate(
            flops=2 * 2 * TOK * D * KVW, bytes_accessed=40 * MIB, transcendentals=0
        ),
    )(gain, ahead, behind, weight)


def dot(a, b):
    return jnp.dot(a, b, preferred_element_type=F32)


def dot_t(a, b):
    return lax.dot_general(a, b, (((1,), (1,)), ((), ())), preferred_element_type=F32)


def attention_kernel(
    table,
    keyval_ref,
    ahead_ref,
    behind_ref,
    cotangent_ref,
    out_ref,
    grad_ref,
    terms_ref,
    keys,
    values,
    rows,
    rows_t,
    lifted,
    lifted_t,
    weights,
    summed,
    grad_rows,
    key_sum,
    value_sum,
):
    pair = table[table[RANKS]]

    @pl.loop(0, RANKS)
    def _(rank):
        low = table[rank]
        for part, block in ((0, low), (1, 2 * RANKS - 1 - low)):
            place = pl.ds(pl.multiple_of(block * HALF, HALF), HALF)
            for batch in range(2):
                start = batch * TOK + part * HALF
                source = keyval_ref[rank, start : start + HALF, :]
                keys[batch, place, :] = source[:, :DH]
                values[batch, place, :DH] = source[:, DH:]

    for batch in range(2):
        values[batch, :, DH:] = jnp.ones((SEQ, DH), BF16)
    key_sum[...] = jnp.zeros_like(key_sum)
    value_sum[...] = jnp.zeros_like(value_sum)
    tiles = HALF * HQ // TILE

    def stack(source, part):
        picked = source[part * HALF : (part + 1) * HALF, :]
        return jnp.concatenate([picked[:, h * DH : (h + 1) * DH] for h in range(HQ)], axis=0)

    def unstack(target, part, block):
        for h in range(HQ):
            target[part * HALF : (part + 1) * HALF, h * DH : (h + 1) * DH] = block[
                h * HALF : (h + 1) * HALF
            ].astype(BF16)

    for part in range(2):
        block = pair if part == 0 else 2 * RANKS - 1 - pair
        last = block // (CHUNK // HALF)
        row_place = block * HALF

        def weigh(batch, j, masked):
            columns = pl.ds(pl.multiple_of(j * CHUNK, CHUNK), CHUNK)
            for t in range(tiles):
                mine = slice(t * TILE, (t + 1) * TILE)
                scores = dot_t(rows[mine, :], keys[batch, columns, :])
                found = jnp.exp2(scores * EXP_SCALE)
                if masked:
                    shape = (TILE, CHUNK)
                    row_at = lax.broadcasted_iota(jnp.int32, shape, 0) % HALF + row_place
                    key_at = lax.broadcasted_iota(jnp.int32, shape, 1) + j * CHUNK
                    found = jnp.where(key_at <= row_at, found, 0.0)
                found = found.astype(BF16)
                if batch == 1:
                    weights[mine, columns] = found
                summed[mine, :] += dot(found, values[batch, columns, :])

        def weigh_all(batch):
            summed[...] = jnp.zeros_like(summed)

            @pl.loop(0, last)
            def _(j):
                weigh(batch, j, False)

            weigh(batch, last, True)

        rows[...] = stack(ahead_ref, part)
        weigh_all(0)
        unstack(out_ref, part, summed[:, :DH] / summed[:, DH:])

        rows[...] = stack(behind_ref, part)
        weigh_all(1)
        cotangent = stack(cotangent_ref, part).astype(F32)
        inverse = 1.0 / summed[:, DH:]
        delta = jnp.sum(cotangent * summed[:, :DH] * inverse, axis=1, keepdims=True) * inverse
        lane = lax.broadcasted_iota(jnp.int32, delta.shape, 1)
        first = delta.astype(BF16).astype(F32)
        second = (delta - first).astype(BF16).astype(F32)
        third = delta - first - second
        split = jnp.where(lane == 0, first, jnp.where(lane == 1, second, jnp.where(lane == 2, third, 0.0)))
        lift = cotangent * inverse
        lifted[:, :DH] = lift.astype(BF16)
        lifted[:, DH:] = (-split).astype(BF16)
        rows_t[...] = rows[...].astype(F32).T.astype(BF16)
        lifted_t[...] = lift.T.astype(BF16)
        grad_rows[...] = jnp.zeros_like(grad_rows)

        @pl.loop(0, last + 1)
        def _(j):
            columns = pl.ds(pl.multiple_of(j * CHUNK, CHUNK), CHUNK)
            for t in range(tiles):
                mine = slice(t * TILE, (t + 1) * TILE)
                found = weights[mine, columns]
                slope = dot_t(lifted[mine, :], values[1, columns, :])
                slope = (found.astype(F32) * slope).astype(BF16)
                grad_rows[mine, :] += dot(slope, keys[1, columns, :])
                key_sum[:, columns] += dot(rows_t[:, mine], slope)
                value_sum[:, columns] += dot(lifted_t[:, mine], found)

        unstack(grad_ref, part, grad_rows[...] * SCALE)

    for j in range(SEQ // CHUNK):
        place = slice(j * CHUNK, (j + 1) * CHUNK)
        keys[0, place, :] = (key_sum[:, place] * SCALE).T.astype(BF16)
        keys[1, place, :] = value_sum[:, place].T.astype(BF16)

    @pl.loop(0, RANKS)
    def _(rank):
        low = table[rank]
        for part, block in ((0, low), (1, 2 * RANKS - 1 - low)):
            place = pl.ds(pl.multiple_of(block * HALF, HALF), HALF)
            for which in range(2):
                terms_ref[rank, part * HALF : (part + 1) * HALF, which * DH : (which + 1) * DH] = keys[
                    which, place, :
                ]


def attention_call(table, keyval, ahead, behind, cotangent):
    vmem_spec = pl.BlockSpec(memory_space=pltpu.VMEM)
    many = HALF * HQ
    return pl.pallas_call(
        attention_kernel,
        name="attention",
        out_shape=(
            jax.ShapeDtypeStruct((TOK, HQ * DH), BF16),
            jax.ShapeDtypeStruct((TOK, HQ * DH), BF16),
            jax.ShapeDtypeStruct((RANKS, TOK, KVW), BF16),
        ),
        in_specs=[pl.BlockSpec(memory_space=pltpu.SMEM)] + [vmem_spec] * 4,
        out_specs=(vmem_spec,) * 3,
        scratch_shapes=[
            pltpu.VMEM((2, SEQ, DH), BF16),
            pltpu.VMEM((2, SEQ, KVW), BF16),
            pltpu.VMEM((many, DH), BF16),
            pltpu.VMEM((DH, many), BF16),
            pltpu.VMEM((many, KVW), BF16),
            pltpu.VMEM((DH, many), BF16),
            pltpu.VMEM((many, SEQ), BF16),
            pltpu.VMEM((many, KVW), F32),
            pltpu.VMEM((many, DH), F32),
            pltpu.VMEM((DH, SEQ), F32),
            pltpu.VMEM((DH, SEQ), F32),
        ],
        compiler_params=pltpu.CompilerParams(vmem_limit_bytes=50 * MIB),
        cost_estimate=pl.CostEstimate(
            flops=8 * 2 * TOK * HQ * SEQ * DH // 2,
            bytes_accessed=8 * MIB,
            transcendentals=TOK * HQ * SEQ,
        ),
    )(table, keyval, ahead, behind, cotangent)


def sum_kernel(
    terms_ref,
    pair_ref,
    key_grad_out,
    weight_grad_out,
    terms,
    pairs,
    both,
    both_t,
    products,
    term_got,
    product_got,
    load_sems,
    send_sems,
    term_recv,
    both_recv,
    product_recv,
):
    place = Place()
    sender = Sender(send_sems)
    loads = [
        pltpu.make_async_copy(terms_ref, terms, load_sems.at[0]),
        pltpu.make_async_copy(pair_ref, pairs, load_sems.at[1]),
    ]
    for load in loads:
        load.start()
    place.barrier()
    loads[0].wait()
    key_grads = ring_sum(
        place, sender, lambda slot: terms.at[slot], term_got, term_recv, lambda unused: None
    ).astype(BF16)
    key_grad_out[...] = key_grads
    mine = pl.ds(pl.multiple_of(place.core * TOK, TOK), TOK)
    theirs = pl.ds(pl.multiple_of((1 - place.core) * TOK, TOK), TOK)
    both[mine, :] = key_grads
    sender.push(both.at[mine], both.at[mine], both_recv, place.sibling())
    loads[1].wait()
    sender.landed(both.at[theirs], both_recv, place.sibling())
    both_t[...] = both[...].astype(F32).T.astype(BF16)

    def make(slot):
        products[slot] = dot(both_t[...], pairs[slot]).astype(BF16)

    weight_grad = ring_sum(place, sender, lambda slot: products.at[slot], product_got, product_recv, make)
    weight_grad_out[...] = weight_grad.T
    sender.finish()


def sum_call(terms, pair_normed):
    any_spec = pl.BlockSpec(memory_space=pl.ANY)
    vmem_spec = pl.BlockSpec(memory_space=pltpu.VMEM)
    return pl.pallas_call(
        sum_kernel,
        name="sum_grads",
        out_shape=(
            jax.ShapeDtypeStruct((TOK, KVW), BF16),
            jax.ShapeDtypeStruct((KVW, KVW), F32),
        ),
        in_specs=[any_spec, any_spec],
        out_specs=(vmem_spec, vmem_spec),
        scratch_shapes=[
            pltpu.VMEM((RANKS, TOK, KVW), BF16),
            pltpu.VMEM((RANKS, KVW, KVW), BF16),
            pltpu.VMEM((2 * TOK, KVW), BF16),
            pltpu.VMEM((KVW, 2 * TOK), BF16),
            pltpu.VMEM((RANKS, KVW, KVW), BF16),
            pltpu.VMEM((31, TOK, KVW), BF16),
            pltpu.VMEM((31, KVW, KVW), BF16),
            pltpu.SemaphoreType.DMA((2,)),
            pltpu.SemaphoreType.DMA((64,)),
            pltpu.SemaphoreType.DMA((31,)),
            pltpu.SemaphoreType.DMA,
            pltpu.SemaphoreType.DMA((31,)),
        ],
        compiler_params=pltpu.CompilerParams(
            collective_id=1, has_side_effects=True, vmem_limit_bytes=50 * MIB
        ),
        cost_estimate=pl.CostEstimate(
            flops=2 * 2 * TOK * D * KVW // 2, bytes_accessed=20 * MIB, transcendentals=0
        ),
    )(terms, pair_normed)


BLOCKS = 4


def stream_kernel(*refs):
    out_ref = refs[-1]
    result = None
    for s in range(2):
        hidden_ref, weight_ref, gain_ref, grads_ref, stat_ref = refs[s * 5 : s * 5 + 5]
        grads = grads_ref[...]
        inverse = stat_ref[0]
        inner = jnp.sum(grads.astype(F32) * stat_ref[1], axis=1, keepdims=True) * (1.0 / D)
        share = inverse * inverse * inner
        pieces = []
        for k in range(BLOCKS):
            columns = slice(k * KVW, (k + 1) * KVW)
            grown = dot_t(grads, weight_ref[columns, :]) * gain_ref[:, columns]
            pieces.append(inverse * grown - hidden_ref[:, columns].astype(F32) * share)
        if s == 0:
            result = pieces
        else:
            result = [a + b.astype(BF16).astype(F32) for a, b in zip(result, pieces)]
    for k in range(BLOCKS):
        out_ref[:, k * KVW : (k + 1) * KVW] = result[k].astype(BF16)


def stream_call(own, later):
    wide = BLOCKS * KVW
    specs = [
        pl.BlockSpec((TOK, wide), lambda i: (0, i)),
        pl.BlockSpec((wide, KVW), lambda i: (i, 0)),
        pl.BlockSpec((1, wide), lambda i: (0, i)),
        pl.BlockSpec((TOK, KVW), lambda i: (0, 0)),
        pl.BlockSpec((2, TOK, KVW), lambda i: (0, 0, 0)),
    ]
    return pl.pallas_call(
        stream_kernel,
        name="stream",
        grid=(D // wide,),
        out_shape=jax.ShapeDtypeStruct((TOK, D), BF16),
        in_specs=specs * 2,
        out_specs=pl.BlockSpec((TOK, wide), lambda i: (0, i)),
        compiler_params=pltpu.CompilerParams(vmem_limit_bytes=40 * MIB),
        cost_estimate=pl.CostEstimate(
            flops=2 * 2 * TOK * D * KVW, bytes_accessed=28 * MIB, transcendentals=0
        ),
    )(*own, *later)


def shifted(x):
    return lax.ppermute(x, "pipe", [(1, 0)])


def body(
    ahead_hidden,
    ahead_queries,
    behind_hidden,
    behind_queries,
    behind_cotangent,
    keyval_weight,
    norm_gain,
    pair_of_rank,
):
    ctx_index = lax.axis_index("ctx")
    gain = norm_gain[0].astype(F32)
    behind = behind_hidden[0, 0]
    later_hidden = shifted(behind)
    later_gain = shifted(norm_gain).astype(F32)
    later_weight = lax.all_gather(shifted(keyval_weight[0]), ("ctx", "dp"), axis=0, tiled=True)
    weight, keyval, pair_normed, stats = gather_call(
        gain.reshape(D // KVW, 1, KVW), ahead_hidden[0, 0], behind, keyval_weight[0]
    )
    later_stats = shifted(stats)
    table = jnp.concatenate([pair_of_rank, ctx_index[None].astype(jnp.int32)])
    attention_out, query_grad, terms = attention_call(
        table, keyval, ahead_queries[0, 0], behind_queries[0, 0], behind_cotangent[0, 0]
    )
    key_grads, weight_grad = sum_call(terms, pair_normed)
    later_grads = shifted(key_grads)
    stream = stream_call(
        (behind, weight.reshape(D, KVW), gain.reshape(1, D), key_grads, stats),
        (later_hidden, later_weight, later_gain, later_grads, later_stats),
    )
    return (
        attention_out[None, None],
        query_grad[None, None],
        stream[None, None],
        weight_grad[None],
    )


def solution(mesh):
    in_specs = (
        P("pipe", "dp", "ctx", None),
        P("pipe", "dp", "ctx", None),
        P("pipe", "dp", "ctx", None),
        P("pipe", "dp", "ctx", None),
        P("pipe", "dp", "ctx", None),
        P("pipe", ("ctx", "dp"), None),
        P("pipe", None),
        P(),
    )
    out_specs = (
        P("pipe", "dp", "ctx", None),
        P("pipe", "dp", "ctx", None),
        P("pipe", "dp", "ctx", None),
        P("pipe", ("ctx", "dp"), None),
    )
    return jax.shard_map(body, mesh=mesh, in_specs=in_specs, out_specs=out_specs, check_vma=False)
```

time: 897 us -> 317 us (0.35)
  waiting for transfers between devices: 700 us -> 4.74 us
  Pallas kernels: 0 us -> 277 us
  matrix products: 116 us -> 0 us
  other arithmetic: 35.3 us -> 1.05 us
  local copies, waits for them, and re-layouts: 24 us -> 4.46 us
    reduce_scatter x2 -> x0, waiting for transfers between devices: 498 us -> none  [the longest x1 319 us: body(): lax.psum_scatter(partial_grad, ('ctx', 'dp'), scatter_dimension=0, tiled=...]
    pallas_call x0 -> x4, Pallas kernels: none -> 277 us  [the longest x1 166 us: gather_call(): pl.pallas_call(gather_kernel, name='gather_project', out_shape=(jax.Shape...]
    all_gather x3 -> x1, waiting for transfers between devices: 200 us -> 0.02 us  [body(): lax.all_gather(shifted(keyval_weight[0]), ('ctx', 'dp'), axis=0, tiled=True)]
    dot_general x34 -> x0, matrix products: 116 us -> none  [the longest x9 31.4 us: masked_weights(): lax.dot_general(query_rows, key_rows, (((1,), (1,)), ((), ())), preferred...]
    broadcast_in_dim x6 -> x0, other arithmetic: 9.36 us -> none  [the longest x1 9.03 us: body(): stream_grad[None, None]]
  transfers between devices with their start and end apart: 6 -> 6, of which waited for: 6 -> 2; matrix products, arithmetic and copies ran while one was open for 9% -> 0% of each run, Pallas kernels for 0% -> 83%
where the time goes in v1:
time: 317 us; the launch traced here: 313 us
  Pallas kernels  277 us (87%)
  between operations  14.2 us (4%)
  starting transfers between devices  12.1 us (4%)
  waiting for transfers between devices  4.74 us (1%)
  local copies, waits for them, and re-layouts  4.46 us (1%)
    pallas_call x1, Pallas kernels, gather_call(): pl.pallas_call(gather_kernel, name='gather_project', out_shape=(jax.Shape...  166 us
    pallas_call x1, Pallas kernels, sum_call(): pl.pallas_call(sum_kernel, name='sum_grads', out_shape=(jax.ShapeDtypeStr...  58.7 us
    pallas_call x1, Pallas kernels, attention_call(): pl.pallas_call(attention_kernel, name='attention', out_shape=(jax.ShapeDt...  34.9 us
    pallas_call x1, Pallas kernels, stream_call(): pl.pallas_call(stream_kernel, name='stream', grid=(D // wide,), out_shape...  17.3 us
    ppermute x5, starting transfers between devices, shifted(): return lax.ppermute(x, 'pipe', [(1, 0)])  12 us
  transfers between devices with their start and end apart: 6, of which 2 were waited for; matrix products, arithmetic and copies ran while one was open for 0% of the time, Pallas kernels for 83%

profile of v1, /device:TPU:32, one launch (start us, length us, event | category | flops | bytes accessed | tf_op | source)
XLA Modules:
  0.0 313.3 jit_solution(16052911467787945680)
XLA Ops:
  7.2 0.0 all-gather.2.cloned.1.call-start
  7.2 1.9 collective-permute-start.1
  9.2 2.8 collective-permute-done.1
  12.0 0.0 copy-start.5
  12.0 0.7 copy-done.5
  12.6 0.0 all-gather.2.cloned.1.call-update
  12.6 6.2 %collective-permute-start = (bf16[128,16384]{1,0:T(8,128)(2,1)}, bf16[128,16384]{1,0:T(8,128)(2,1)}, u32[]{:S(2)}, u32[]{:S(2)}) collective-permute-start(bf16[128,16384]{1,0:T(8,128)(2,1)} %bitcast.13), channel_id=1, source_target_pairs={{64,0},{65,1},{66,2},{67,3},{68,4},{69,5},{70,6},{71,7},{72,8},{73... | collective-permute-start | bytes 12582920 | tf_op jit(solution)/shard_map/ppermute | solution.py:708
  18.9 0.9 convert_element_type.23.refs_2_
  19.8 0.0 copy-start.1
  19.8 0.9 copy-done.1
  20.7 0.0 copy-start.7
  20.7 0.0 copy-start.2
  20.7 0.0 copy-start.3
  20.7 0.0 copy-start.4
  20.7 165.9 %gather_project.1 = (bf16[32,2,256,256]{3,2,1,0:T(8,128)(2,1)}, bf16[32,256,256]{2,1,0:T(8,128)(2,1)}, bf16[32,256,256]{2,1,0:T(8,128)(2,1)}, f32[2,128,256]{2,1,0:T(8,128)S(1)}) custom-call(f32[64,1,256]{2,1,0:T(1,128)S(1)} %bitcast.16, bf16[128,16384]{1,0:T(8,128)(2,1)} %bitcast.25, bf16[128,16384]{1,0:T(8,128)(2,1)} %bitcast.14, bf16[256,256]{1,0:T(8,128)(2,1)S(1)} %bitcast.19), custom_call_target="tpu_custom_call" | custom-call | flops 2147483648 | bytes 41943040 | tf_op jit(solution)/shard_map/gather_project/pallas_call | solution.py:369
  186.6 1.3 collective-permute-start.4
  187.9 0.0 copy-done.7
  187.9 0.1 pad_add_fusion.table
  188.0 0.0 copy-done.2
  188.0 0.0 copy-done.3
  188.0 0.0 copy-done.4
  188.0 34.9 %attention.1 = (bf16[128,2048]{1,0:T(8,128)(2,1)}, bf16[128,2048]{1,0:T(8,128)(2,1)}, bf16[32,128,256]{2,1,0:T(8,128)(2,1)S(1)}) custom-call(s32[33]{0:T(128)S(1)} %pad_add_fusion.table, bf16[32,256,256]{2,1,0:T(8,128)(2,1)} %get-tuple-element.13.keyval_ref, bf16[128,2048]{1,0:T(8,128)(2,1)S(1)} %bitcast.20, bf16[128,2048]{1,0:T(8,128)(2,1)S(1)} %bitcast.21, ...), custom_call_target="tpu_custom_call" | custom-call | flops 8589934592 | bytes 8388608 | tf_op jit(solution)/shard_map/attention/pallas_call | solution.py:544
  222.9 0.0 copy-start.6
  222.9 58.7 %sum_grads.1 = (bf16[128,256]{1,0:T(8,128)(2,1)S(1)}, f32[256,256]{1,0:T(8,128)S(1)}) custom-call(bf16[32,128,256]{2,1,0:T(8,128)(2,1)S(1)} %get-tuple-element.17.terms_ref, bf16[32,256,256]{2,1,0:T(8,128)(2,1)} %get-tuple-element.18.pair_ref), custom_call_target="tpu_custom_call" | custom-call | flops 1073741824 | bytes 20971520 | tf_op jit(solution)/shard_map/sum_grads/pallas_call | solution.py:627
  281.6 1.3 collective-permute-start.3
  282.9 0.0 copy-done.6
  282.9 1.3 collective-permute-start.2
  284.2 1.9 collective-permute-done.2
  286.1 0.1 convert_element_type.22.refs_7_
  286.2 0.0 collective-permute-done.3.refs_8_
  286.2 0.0 collective-permute-done.4.refs_9_
  286.2 0.0 collective-permute-done.refs_5_
  286.2 0.0 all-gather.2.cloned.1.call-done.refs_6_
  286.2 0.0 copy-start
  286.2 2.2 copy-done
  288.4 17.3 %stream.1 = bf16[128,16384]{1,0:T(8,128)(2,1)} custom-call(bf16[128,16384]{1,0:T(8,128)(2,1)S(1)} %bitcast.15, bf16[16384,256]{1,0:T(8,128)(2,1)} %bitcast.23, f32[1,16384]{1,0:T(1,128)S(1)} %convert_element_type.23.refs_2_, bf16[128,256]{1,0:T(8,128)(2,1)S(1)} %get-tuple-element.19.refs_3_, f32[2,128,256]{2,1,0:T(8,128)S(1)} %get-tuple-element.20.refs_4_, ...), custom_call_target="tpu_custom_call" | custom-call | flops 2147483648 | bytes 29360128 | tf_op jit(solution)/shard_map/stream/pallas_call | solution.py:693
  305.7 0.7 copy.14
Async XLA Ops:
  7.2 279.1 %all-gather.2.cloned.1.call-start = ((), (), s32[]{:S(2)}) async-start(), calls=%async_computation | async-start | bytes 8519680 | tf_op jit(solution)/shard_map/all_gather | solution.py:726
  7.2 4.8 %collective-permute-start.1 = (bf16[256,256]{1,0:T(8,128)(2,1)}, bf16[256,256]{1,0:T(8,128)(2,1)S(1)}, u32[]{:S(2)}, u32[]{:S(2)}) collective-permute-start(bf16[256,256]{1,0:T(8,128)(2,1)} %bitcast.18), channel_id=1, source_target_pairs={{64,0},{65,1},{66,2},{67,3},{68,4},{69,5},{70,6},{71,7},{72,8},{73... | collective-permute-start | bytes 393224 | tf_op jit(solution)/shard_map/ppermute | solution.py:708
  12.0 0.7 copy-start.5
  12.6 273.6 %collective-permute-start = (bf16[128,16384]{1,0:T(8,128)(2,1)}, bf16[128,16384]{1,0:T(8,128)(2,1)}, u32[]{:S(2)}, u32[]{:S(2)}) collective-permute-start(bf16[128,16384]{1,0:T(8,128)(2,1)} %bitcast.13), channel_id=1, source_target_pairs={{64,0},{65,1},{66,2},{67,3},{68,4},{69,5},{70,6},{71,7},{72,8},{73... | collective-permute-start | bytes 12582920 | tf_op jit(solution)/shard_map/ppermute | solution.py:708
  19.8 0.9 copy-start.1
  20.7 167.3 %copy-start.7 = (s32[32]{0:T(128)S(1)}, s32[32]{0:T(128)}, u32[]{:S(2)}) copy-start(s32[32]{0:T(128)} %param.15) | copy-start | bytes 388
  20.7 167.3 %copy-start.2 = (bf16[1,1,128,2048]{3,2,1,0:T(8,128)(2,1)S(1)}, bf16[1,1,128,2048]{3,2,1,0:T(8,128)(2,1)}, u32[]{:S(2)}) copy-start(bf16[1,1,128,2048]{3,2,1,0:T(8,128)(2,1)} %param.9) | copy-start | bytes 1572868
  20.7 167.3 %copy-start.3 = (bf16[1,1,128,2048]{3,2,1,0:T(8,128)(2,1)S(1)}, bf16[1,1,128,2048]{3,2,1,0:T(8,128)(2,1)}, u32[]{:S(2)}) copy-start(bf16[1,1,128,2048]{3,2,1,0:T(8,128)(2,1)} %param.11) | copy-start | bytes 1572868
  20.7 167.3 %copy-start.4 = (bf16[1,1,128,2048]{3,2,1,0:T(8,128)(2,1)S(1)}, bf16[1,1,128,2048]{3,2,1,0:T(8,128)(2,1)}, u32[]{:S(2)}) copy-start(bf16[1,1,128,2048]{3,2,1,0:T(8,128)(2,1)} %param.12) | copy-start | bytes 1572868
  186.6 99.6 %collective-permute-start.4 = (f32[2,128,256]{2,1,0:T(8,128)S(1)}, f32[2,128,256]{2,1,0:T(8,128)S(1)}, u32[]{:S(2)}, u32[]{:S(2)}) collective-permute-start(f32[2,128,256]{2,1,0:T(8,128)S(1)} %get-tuple-element.20.refs_4_), channel_id=1, source_target_pairs={{64,0},{65,1},{66,2},{67,3},{68,4},{69,5},{70,6},{71,7},{72,8},{73... | collective-permute-start | bytes 786440 | tf_op jit(solution)/shard_map/ppermute | solution.py:708
  222.9 60.0 %copy-start.6 = (bf16[1,16384]{1,0:T(2,128)(2,1)S(1)}, bf16[1,16384]{1,0:T(2,128)(2,1)}, u32[]{:S(2)}) copy-start(bf16[1,16384]{1,0:T(2,128)(2,1)} %param.14) | copy-start | bytes 98308
  281.6 4.6 %collective-permute-start.3 = (bf16[128,256]{1,0:T(8,128)(2,1)S(1)}, bf16[128,256]{1,0:T(8,128)(2,1)S(1)}, u32[]{:S(2)}, u32[]{:S(2)}) collective-permute-start(bf16[128,256]{1,0:T(8,128)(2,1)S(1)} %get-tuple-element.19.refs_3_), channel_id=1, source_target_pairs={{64,0},{65,1},{66,2},{67,3},{68,4},{69,5},{70,6},{71,7},{72,8},{73... | collective-permute-start | bytes 196616 | tf_op jit(solution)/shard_map/ppermute | solution.py:708
  282.9 3.2 %collective-permute-start.2 = (bf16[1,16384]{1,0:T(2,128)(2,1)S(1)}, bf16[1,16384]{1,0:T(2,128)(2,1)S(1)}, u32[]{:S(2)}, u32[]{:S(2)}) collective-permute-start(bf16[1,16384]{1,0:T(2,128)(2,1)S(1)} %copy-done.6), channel_id=1, source_target_pairs={{64,0},{65,1},{66,2},{67,3},{68,4},{69,5},{70,6},{71,7},{72,8},{73... | collective-permute-start | bytes 98312 | tf_op jit(solution)/shard_map/ppermute | solution.py:708
  286.2 2.2 copy-start
Sparse Core Ops, SparseCore 0:
  12.8 106.5 all-gather.1

commit v2 on v1

v2 whole, which is shorter than its diff:
```python
import jax
import jax.numpy as jnp
import numpy as np
from jax import lax
from jax.experimental import pallas as pl
from jax.experimental.pallas import tpu as pltpu
from jax.sharding import PartitionSpec as P

D = 16384
DH = 128
HQ = 16
TOK = 128
KVW = 256
RANKS = 32
SEQ = RANKS * TOK
HALF = TOK // 2
CHUNK = 512
NORM_EPS = 1e-05
SCALE = DH ** (-0.5)
EXP_SCALE = SCALE * 1.4426950408889634
F32 = jnp.float32
BF16 = jnp.bfloat16
MESH = pl.DeviceIdType.MESH
MIB = 1024 * 1024

ORDER = ((0, 0), (0, 1), (-1, 0), (1, 0), (-1, 1), (1, 1), (2, 0), (2, 1))


def rid(du, dv, zr):
    return ((dv % 4) * 4 + du % 4) * 2 + zr


class Place:
    def __init__(self):
        self.pipe = lax.axis_index("pipe")
        ctx = lax.axis_index("ctx")
        core = lax.axis_index("dp")
        y, z, x = ctx // 8, (ctx // 4) % 2, ctx % 4
        self.ctx, self.core, self.z = ctx, core, z
        self.u = x * (1 - core) + y * core
        self.v = y * (1 - core) + x * core
        self.su = 1 + 7 * core
        self.sv = 8 - 7 * core

    def slot(self, du, dv, zr):
        z = self.z if zr == 0 else 1 - self.z
        return ((self.u + du + 4) % 4) * self.su + ((self.v + dv + 4) % 4) * self.sv + z * 4

    def sibling_slot(self, du, dv, zr):
        z = self.z if zr == 0 else 1 - self.z
        return ((self.v + du + 4) % 4) * self.sv + ((self.u + dv + 4) % 4) * self.su + z * 4

    def device(self, du, dv, zr):
        return (self.pipe, self.slot(du, dv, zr), self.core)

    def sibling(self):
        return (self.pipe, self.ctx, 1 - self.core)

    def section_mate(self):
        return (1 - self.pipe, self.ctx, self.core)

    def barrier(self):
        semaphore = pltpu.get_barrier_semaphore()
        partners = [
            self.device(0, 0, 1),
            self.device(1, 0, 0),
            self.device(-1, 0, 0),
            self.device(0, 1, 0),
            self.device(0, -1, 0),
            self.sibling(),
            self.section_mate(),
        ]
        for partner in partners:
            pl.semaphore_signal(semaphore, inc=1, device_id=partner, device_id_type=MESH)
        pl.semaphore_wait(semaphore, len(partners))


class Sender:
    def __init__(self, send_sems, base=0):
        self.send_sems = send_sems
        self.base = base
        self.copies = []

    def push(self, src, dst, recv_sem, device):
        copy = pltpu.make_async_remote_copy(
            src_ref=src,
            dst_ref=dst,
            send_sem=self.send_sems.at[self.base + len(self.copies)],
            recv_sem=recv_sem,
            device_id=device,
            device_id_type=MESH,
        )
        copy.start()
        self.copies.append(copy)

    def landed(self, dst, recv_sem, device):
        pltpu.make_async_remote_copy(
            src_ref=dst,
            dst_ref=dst,
            send_sem=self.send_sems.at[0],
            recv_sem=recv_sem,
            device_id=device,
            device_id_type=MESH,
        ).wait_recv()

    def finish(self):
        for copy in self.copies:
            copy.wait_send()


def ring_gather(place, sender, at, recv, to_sibling):
    z_mate = place.device(0, 0, 1)
    u_right, u_left = place.device(1, 0, 0), place.device(-1, 0, 0)
    v_right, v_left = place.device(0, 1, 0), place.device(0, -1, 0)

    def send(slot, seen, device):
        sender.push(at(slot), at(slot), recv.at[rid(*seen)], device)

    def wait(du, dv, zr):
        slot = place.slot(du, dv, zr)
        sender.landed(at(slot), recv.at[rid(du, dv, zr)], z_mate)
        return slot

    own = place.slot(0, 0, 0)
    send(own, (0, 0, 1), z_mate)
    send(own, (-1, 0, 0), u_right)
    send(own, (1, 0, 0), u_left)
    send(own, (0, -1, 0), v_right)
    send(own, (0, 1, 0), v_left)
    to_sibling(own, 0, 0, 0)
    yield own
    for du, zr in ORDER[1:]:
        slot = wait(du, 0, zr)
        if du == 0:
            send(slot, (-1, 0, 1), u_right)
            send(slot, (1, 0, 1), u_left)
        elif du == -1 and zr == 0:
            send(slot, (2, 0, 0), u_right)
        elif du == 1 and zr == 1:
            send(slot, (2, 0, 1), u_left)
        send(slot, (du, -1, zr), v_right)
        send(slot, (du, 1, zr), v_left)
        to_sibling(slot, du, 0, zr)
        yield slot
    for du, zr in ORDER:
        for dv in (-1, 1):
            slot = wait(du, dv, zr)
            if dv == -1 and zr == 0:
                send(slot, (du, 2, 0), v_right)
            elif dv == 1 and zr == 1:
                send(slot, (du, 2, 1), v_left)
            to_sibling(slot, du, dv, zr)
            yield slot
    for du, zr in ORDER:
        slot = wait(du, 2, zr)
        to_sibling(slot, du, 2, zr)
        yield slot


SIBLING_ORDER = [(du, 0, zr) for du, zr in ORDER]
SIBLING_ORDER += [(du, dv, zr) for du, zr in ORDER for dv in (-1, 1)]
SIBLING_ORDER += [(du, 2, zr) for du, zr in ORDER]


def no_sibling(*unused):
    pass


def ring_sum(place, sender, term, got, recv, make, result):
    z_mate = place.device(0, 0, 1)
    u_right, u_left = place.device(1, 0, 0), place.device(-1, 0, 0)
    v_right, v_left = place.device(0, 1, 0), place.device(0, -1, 0)

    def send(slot, index, device):
        sender.push(term(slot), got(index), recv.at[index], device)

    def wait(index):
        sender.landed(got(index), recv.at[index], z_mate)
        return got(index)[...].astype(F32)

    def add(slot, *indices):
        total = term(slot)[...].astype(F32)
        for index in indices:
            total = total + wait(index)
        term(slot)[...] = total.astype(BF16)

    far = (2, -1, 1, 0)
    for k, du in enumerate(far):
        slot = place.slot(du, 2, 0)
        make(slot)
        send(slot, k, v_right)
        slot = place.slot(du, 2, 1)
        make(slot)
        send(slot, 4 + k, v_left)
    for k, du in enumerate(far):
        slot = place.slot(du, 1, 1)
        make(slot)
        send(slot, 8 + 2 * k + 1, v_right)
        slot = place.slot(du, -1, 0)
        make(slot)
        send(slot, 16 + 2 * k, v_left)
    for du in far:
        make(place.slot(du, 1, 0))
        make(place.slot(du, -1, 1))
    yield
    for k, du in enumerate(far):
        slot = place.slot(du, 1, 0)
        add(slot, k)
        send(slot, 8 + 2 * k, v_right)
        slot = place.slot(du, -1, 1)
        add(slot, 4 + k)
        send(slot, 16 + 2 * k + 1, v_left)
        yield
    for du in far:
        for zr in (0, 1):
            make(place.slot(du, 0, zr))
    for k, du in enumerate(far):
        for zr in (1, 0):
            add(place.slot(du, 0, zr), 8 + 2 * k + zr, 16 + 2 * k + zr)
        if du == 2:
            send(place.slot(2, 0, 0), 24, u_right)
            send(place.slot(2, 0, 1), 25, u_left)
        elif du == -1:
            send(place.slot(-1, 0, 0), 28, u_left)
            add(place.slot(-1, 0, 1), 25)
            send(place.slot(-1, 0, 1), 29, u_left)
        elif du == 1:
            send(place.slot(1, 0, 1), 27, u_right)
            add(place.slot(1, 0, 0), 24)
            send(place.slot(1, 0, 0), 26, u_right)
        yield
    other = place.slot(0, 0, 1)
    add(other, 27, 29)
    send(other, 30, z_mate)
    yield
    total = term(place.slot(0, 0, 0))[...].astype(F32)
    for index in (26, 28, 30):
        total = total + wait(index)
    result.append(total)


def dot(a, b):
    return jnp.dot(a, b, preferred_element_type=F32)


def dot_t(a, b):
    return lax.dot_general(a, b, (((1,), (1,)), ((), ())), preferred_element_type=F32)


ITEMS = SEQ // CHUNK + 1
LOW_ITEMS = RANKS * HALF // CHUNK
PER_CHUNK = CHUNK // HALF


def item_tables():
    lines = []
    for pair in range(RANKS):
        last = pair // PER_CHUNK
        parts = [0 if i <= last else 1 for i in range(ITEMS)]
        chunks = [i if i <= last else i - last - 1 for i in range(ITEMS)]
        starts = [(pair if part == 0 else 2 * RANKS - 1 - pair) * HALF for part in parts]
        line = parts + [chunk * PER_CHUNK for chunk in chunks]
        line += [chunk * CHUNK - start for chunk, start in zip(chunks, starts)]
        line += [min(last + 1 + j, ITEMS - 1) for j in range(SEQ // CHUNK)]
        line += [int(last + 1 + j <= ITEMS - 1) for j in range(SEQ // CHUNK)]
        line += [int(j <= last) for j in range(SEQ // CHUNK)]
        lines.append(line + [0] * (64 - len(line)))
    return np.array(lines, np.int32)
ROWS = HALF * HQ


def stack(source, part):
    picked = source[part * HALF : (part + 1) * HALF, :]
    return jnp.concatenate([picked[:, h * DH : (h + 1) * DH] for h in range(HQ)], axis=0)


def unstack(target, part, block):
    for h in range(HQ):
        target[part * HALF : (part + 1) * HALF, h * DH : (h + 1) * DH] = block[
            h * HALF : (h + 1) * HALF
        ].astype(BF16)


class Attention:
    def __init__(self, table, rank_of_pair, keys, values, rows, weights, summed):
        self.table, self.rank_of_pair = table, rank_of_pair
        self.keys, self.values, self.rows = keys, values, rows
        self.weights, self.summed = weights, summed

    def order(self, keyval):
        ones = jnp.ones((HALF, DH), BF16)

        @pl.loop(0, RANKS)
        def _(b):
            rank = self.rank_of_pair[b]
            for part, block in ((0, b), (1, 2 * RANKS - 1 - b)):
                source = keyval[rank, part * HALF : (part + 1) * HALF, :]
                self.keys[block] = source[:, :DH]
                self.values[block, :, :DH] = source[:, DH:]
                self.values[block, :, DH:] = ones

    def item(self, i):
        low = None
        part = 1
        if i < LOW_ITEMS:
            part = self.table[i]
            low = lax.broadcast_in_dim(part, (ROWS, DH), ()) == 0
        return low, part, pl.ds(self.table[ITEMS + i], CHUNK // HALF)

    @staticmethod
    def add(target, low, value):
        if low is None:
            target[1] += value
        else:
            if value.shape[1] != low.shape[1]:
                low = jnp.concatenate([low.astype(jnp.int32)] * 2, axis=1) == 1
            target[0] += jnp.where(low, value, 0.0)
            target[1] += jnp.where(low, 0.0, value)

    def weigh(self, i, keep):
        low, part, blocks = self.item(i)
        keys = self.keys[blocks].reshape(CHUNK, DH)
        found = jnp.exp2(dot_t(self.rows[part], keys) * EXP_SCALE)
        if low is not None or i == ITEMS - 1:
            shape = (ROWS, CHUNK)
            ahead = lax.broadcasted_iota(jnp.int32, shape, 0) % HALF - lax.broadcasted_iota(jnp.int32, shape, 1)
            found = jnp.where(ahead >= self.table[2 * ITEMS + i], found, 0.0)
        found = found.astype(BF16)
        if keep:
            for t in range(4):
                self.weights[i * 4 + t] = found[t * 256 : (t + 1) * 256]
        self.add(self.summed, low, dot(found, self.values[blocks].reshape(CHUNK, KVW)))

    def grad(self, i, rows_t, lifted, lifted_t, grad_rows, items):
        low, part, blocks = self.item(i)
        found = jnp.concatenate([self.weights[i * 4 + t] for t in range(4)], axis=0)
        slope = dot_t(lifted[part], self.values[blocks].reshape(CHUNK, KVW))
        slope = (found.astype(F32) * slope).astype(BF16)
        self.add(grad_rows, low, dot(slope, self.keys[blocks].reshape(CHUNK, DH)))
        items[i, :DH, :] = dot(rows_t[part], slope)
        items[i, DH:, :] = dot(lifted_t[part], found)


def whole_kernel(
    table,
    rank_of_pair,
    pair_of_rank,
    gain_ref,
    ahead_ref,
    behind_ref,
    ahead_queries,
    behind_queries,
    cotangent_ref,
    weight_ref,
    out_ref,
    query_grad_ref,
    own_term_out,
    weight_grad_out,
    later_weights_out,
    later_grads_out,
    later_stats_out,
    hidden,
    big,
    weights,
    later_weights,
    keyvals,
    ahead_keyvals,
    pairs,
    keys,
    values,
    items,
    rows,
    rows_t,
    lifted,
    lifted_t,
    summed,
    grad_rows,
    total,
    stats,
    both,
    both_t,
    load_sems,
    send_sems,
    weight_recv,
    sibling_recv,
    later_recv,
    later_sibling_recv,
    keyval_recv,
    ahead_recv,
    term_recv,
    product_recv,
    pair_recv,
    both_recv,
    section_send,
    section_recv,
):
    place = Place()
    sender = Sender(send_sems)
    core, ctx = place.core, place.ctx
    loads = [
        pltpu.make_async_copy(behind_ref, hidden.at[1], load_sems.at[0]),
        pltpu.make_async_copy(ahead_ref, hidden.at[0], load_sems.at[1]),
        pltpu.make_async_copy(weight_ref, weights.at[ctx, core], load_sems.at[2]),
    ]
    loads[2].start()
    loads[0].start()
    loads[1].start()

    is_later = place.pipe == 1
    is_earlier = place.pipe == 0
    crossing = [
        (weight_ref, later_weights.at[ctx, core]),
        (stats, later_stats_out),
        (both.at[pl.ds(pl.multiple_of(core * TOK, TOK), TOK)], later_grads_out),
    ]
    crossings = [
        pltpu.make_async_remote_copy(
            src_ref=src,
            dst_ref=dst,
            send_sem=section_send.at[k],
            recv_sem=section_recv.at[k],
            device_id=place.section_mate(),
            device_id_type=MESH,
        )
        for k, (src, dst) in enumerate(crossing)
    ]
    own_later = pltpu.make_async_copy(weight_ref, later_weights.at[ctx, core], load_sems.at[4])

    place.barrier()
    loads[2].wait()

    @pl.when(is_later)
    def _():
        own_later.start()
        crossings[0].start()
        later_stats_out[...] = jnp.zeros_like(later_stats_out)
        later_grads_out[...] = jnp.zeros_like(later_grads_out)

    total[...] = jnp.zeros_like(total)
    inverses = {}

    def row_scale(batch):
        def step(j, squares):
            block = hidden[batch, :, pl.ds(pl.multiple_of(j * KVW, KVW), KVW)].astype(F32)
            block = block * block
            return squares + block[:, :DH] + block[:, DH:]

        squares = lax.fori_loop(0, D // KVW, step, jnp.zeros((TOK, DH), F32), unroll=4)
        mean = jnp.sum(squares, axis=1, keepdims=True) * (1.0 / D)
        inverses[batch] = lax.rsqrt(mean + NORM_EPS)

    def scale_rows(batch, part):
        inverse = inverses[batch]

        @pl.loop(part * 16, part * 16 + 16)
        def _(i):
            for k in range(2):
                columns = pl.ds(pl.multiple_of((2 * i + k) * KVW, KVW), KVW)
                block = hidden[batch, :, columns].astype(F32) * inverse * gain_ref[2 * i + k]
                big[i, batch * TOK : (batch + 1) * TOK, k * KVW : (k + 1) * KVW] = block.astype(BF16)

    def term_got(k):
        return hidden.at[0, :, pl.ds(k * KVW, KVW)]

    def half(which):
        return pl.ds(pl.multiple_of(which * KVW, KVW), KVW)

    mine = pl.ds(pl.multiple_of(core * TOK, TOK), TOK)
    theirs = pl.ds(pl.multiple_of((1 - core) * TOK, TOK), TOK)
    own_pair = pltpu.make_async_copy(
        big.at[pl.ds(0, RANKS), pl.ds(TOK, TOK), half(core)], pairs.at[:, mine, :], load_sems.at[3]
    )

    def send_pair():
        sender.push(
            big.at[pl.ds(0, RANKS), pl.ds(TOK, TOK), half(1 - core)],
            pairs.at[:, mine, :],
            pair_recv,
            place.sibling(),
        )
        own_pair.start()

    todo = [
        lambda: (loads[0].wait(), row_scale(1)),
        lambda: scale_rows(1, 0),
        lambda: scale_rows(1, 1),
        lambda: (send_pair(), loads[1].wait(), row_scale(0)),
        lambda: scale_rows(0, 0),
        lambda: scale_rows(0, 1),
    ]
    ready = []
    taken = [0]

    def project(slot, which):
        total[...] += dot(big[slot, :, half(which)], weights[slot, which])

    def take_sibling():
        du, dv, zr = SIBLING_ORDER[taken[0]]
        taken[0] += 1
        slot = place.sibling_slot(du, dv, zr)
        sender.landed(weights.at[slot, 1 - core], sibling_recv.at[rid(du, dv, zr)], place.sibling())
        project(slot, 1 - core)

    def relay_to_sibling(buffer, recv):
        def send(slot, du, dv, zr):
            here = buffer.at[slot, core]
            sender.push(here, here, recv.at[rid(du, dv, zr)], place.sibling())

        return send

    first = ring_gather(
        place,
        sender,
        lambda slot: weights.at[slot, core],
        weight_recv,
        relay_to_sibling(weights, sibling_recv),
    )
    for arrived, slot in enumerate(first):
        ready.append(slot)
        if todo:
            todo.pop(0)()
            continue
        while ready:
            project(ready.pop(0), core)
        for _ in range(2):
            if taken[0] < arrived - 1:
                take_sibling()
    while taken[0] < len(SIBLING_ORDER):
        take_sibling()

    keyvals[ctx] = total[TOK:, :].astype(BF16)
    ahead_keyvals[ctx] = total[:TOK, :].astype(BF16)
    stats[0] = jnp.broadcast_to(inverses[1], (TOK, KVW))
    stats[1] = total[TOK:, :]

    def prepare(part):
        rows[part] = stack(behind_queries, part)
        rows_t[part] = rows[part].astype(F32).T.astype(BF16)

    def clear():
        summed[...] = jnp.zeros_like(summed)
        grad_rows[...] = jnp.zeros_like(grad_rows)

    todo = [lambda: prepare(0), lambda: prepare(1), clear]
    for slot in ring_gather(place, sender, lambda slot: keyvals.at[slot], keyval_recv, no_sibling):
        if todo:
            todo.pop(0)()
    second_sends = len(sender.copies)

    @pl.when(is_later)
    def _():
        crossings[1].start()
        own_later.wait()

    @pl.when(is_earlier)
    def _():
        crossings[0].wait_recv()

    ahead_sender = Sender(send_sems, 256)
    ahead = ring_gather(
        place, ahead_sender, lambda slot: ahead_keyvals.at[slot], ahead_recv, no_sibling
    )
    later = ring_gather(
        place,
        sender,
        lambda slot: later_weights.at[slot, core],
        later_recv,
        relay_to_sibling(later_weights, later_sibling_recv),
    )

    def serve(gathers):
        for gather in gathers:
            next(gather, None)

    serve((ahead, later))
    attention = Attention(table, rank_of_pair, keys, values, rows, big, summed)
    attention.order(keyvals)
    for copy in sender.copies[:second_sends]:
        copy.wait_send()
    own_pair.wait()
    for i in range(ITEMS):
        attention.weigh(i, True)
        serve((ahead, later))
    for part in range(2):
        cotangent = stack(cotangent_ref, part).astype(F32)
        inverse = 1.0 / summed[part, :, DH:]
        delta = jnp.sum(cotangent * summed[part, :, :DH] * inverse, axis=1, keepdims=True) * inverse
        lane = lax.broadcasted_iota(jnp.int32, delta.shape, 1)
        one = delta.astype(BF16).astype(F32)
        two = (delta - one).astype(BF16).astype(F32)
        three = delta - one - two
        split = jnp.where(lane == 0, one, jnp.where(lane == 1, two, jnp.where(lane == 2, three, 0.0)))
        lift = cotangent * inverse
        lifted[part, :, :DH] = lift.astype(BF16)
        lifted[part, :, DH:] = (-split).astype(BF16)
        lifted_t[part] = lift.T.astype(BF16)
        serve((ahead, later))
    for i in range(ITEMS):
        attention.grad(i, rows_t, lifted, lifted_t, grad_rows, items)
        serve((ahead, later))

    chunks = SEQ // CHUNK
    for j in range(chunks):
        base = 3 * ITEMS + j
        shape = (KVW, CHUNK)

        def present(at):
            return lax.broadcast_in_dim(table[at], shape, ()) == 1

        found = jnp.where(present(base + chunks), items[table[base]], 0.0)
        if j < LOW_ITEMS:
            found = found + jnp.where(present(base + 2 * chunks), items[j], 0.0)
        found = jnp.concatenate([(found[:DH] * SCALE).T, found[DH:].T], axis=1).astype(BF16)
        values[j * PER_CHUNK : (j + 1) * PER_CHUNK] = found.reshape(PER_CHUNK, HALF, KVW)

    terms = keyvals

    @pl.loop(0, RANKS)
    def _(rank):
        low = pair_of_rank[rank]
        terms[rank, :HALF, :] = values[low]
        terms[rank, HALF:, :] = values[2 * RANKS - 1 - low]

    result = []
    key_sum = ring_sum(
        place,
        sender,
        lambda slot: terms.at[slot],
        term_got,
        term_recv,
        no_sibling,
        result,
    )
    todo = [
        lambda: [unstack(query_grad_ref, part, grad_rows[part] * SCALE) for part in range(2)],
        lambda: [rows.__setitem__(part, stack(ahead_queries, part)) for part in range(2)],
        lambda: summed.__setitem__(Ellipsis, jnp.zeros_like(summed)),
    ]
    for _ in key_sum:
        if todo:
            todo.pop(0)()
        serve((ahead, later))
    key_grads = result[0].astype(BF16)
    both[mine, :] = key_grads
    sender.push(both.at[mine], both.at[mine], both_recv, place.sibling())

    @pl.when(is_later)
    def _():
        crossings[2].start()

    for _ in ahead:
        serve((later,))
    attention.order(ahead_keyvals)
    sender.landed(pairs.at[:, theirs, :], pair_recv, place.sibling())
    sender.landed(both.at[theirs], both_recv, place.sibling())
    both_t[...] = both[...].astype(F32).T.astype(BF16)

    def product(slot):
        return big.at[slot, :, pl.ds(0, KVW)]

    def make(slot):
        product(slot)[...] = dot(both_t[...], pairs[slot]).astype(BF16)

    result = []
    weight_sum = ring_sum(
        place,
        sender,
        product,
        lambda k: big.at[k, :, pl.ds(KVW, KVW)],
        product_recv,
        make,
        result,
    )
    inner = jnp.sum(key_grads.astype(F32) * stats[1], axis=1, keepdims=True) * (1.0 / D)
    inverse = stats[0]
    share = inverse * inverse * inner

    store_later = pltpu.make_async_copy(later_weights, later_weights_out, load_sems.at[5])
    todo = [lambda k=k: [attention.weigh(i, False) for i in range(3 * k, 3 * k + 3)] for k in range(3)]
    todo.append(
        lambda: [unstack(out_ref, p, summed[p, :, :DH] / summed[p, :, DH:]) for p in range(2)]
    )

    def finish_later():
        ahead_sender.finish()
        for _ in later:
            pass
        for du, dv, zr in SIBLING_ORDER:
            slot = place.sibling_slot(du, dv, zr)
            sender.landed(
                later_weights.at[slot, 1 - core], later_sibling_recv.at[rid(du, dv, zr)], place.sibling()
            )

        store_later.start()

    todo.append(finish_later)
    stores = []

    def stream(part):
        @pl.loop(part * 8, part * 8 + 8)
        def _(slot):
            for k in range(2):
                columns = pl.ds(pl.multiple_of((2 * slot + k) * KVW, KVW), KVW)
                grown = dot_t(key_grads, weights[slot, k]) * gain_ref[2 * slot + k]
                own = inverse * grown - hidden[1, :, columns].astype(F32) * share
                hidden[1, :, columns] = own.astype(BF16)

        columns = pl.ds(part * (D // 4), D // 4)
        store = pltpu.make_async_copy(
            hidden.at[1, :, columns], own_term_out.at[:, columns], load_sems.at[6 + part]
        )
        store.start()
        stores.append(store)

    for part in range(4):
        todo.append(lambda part=part: stream(part))
    for _ in weight_sum:
        if todo:
            todo.pop(0)()
        serve((later,))
    weight_grad_out[...] = result[0].T
    while todo:
        todo.pop(0)()
    for store in stores + [store_later]:
        store.wait()
    for copy in sender.copies[second_sends:]:
        copy.wait_send()

    @pl.when(is_later)
    def _():
        for crossing_copy in crossings:
            crossing_copy.wait_send()

    @pl.when(is_earlier)
    def _():
        for crossing_copy in crossings[1:]:
            crossing_copy.wait_recv()


def whole_call(table, rank_of_pair, pair_of_rank, gain, ahead, behind, ahead_queries, behind_queries, cotangent, weight):
    any_spec = pl.BlockSpec(memory_space=pl.ANY)
    vmem_spec = pl.BlockSpec(memory_space=pltpu.VMEM)
    smem_spec = pl.BlockSpec(memory_space=pltpu.SMEM)
    dma = pltpu.SemaphoreType.DMA
    return pl.pallas_call(
        whole_kernel,
        name="layer_window",
        out_shape=(
            jax.ShapeDtypeStruct((TOK, HQ * DH), BF16),
            jax.ShapeDtypeStruct((TOK, HQ * DH), BF16),
            jax.ShapeDtypeStruct((TOK, D), BF16),
            jax.ShapeDtypeStruct((KVW, KVW), F32),
            jax.ShapeDtypeStruct((RANKS, 2, KVW, KVW), BF16),
            jax.ShapeDtypeStruct((TOK, KVW), BF16),
            jax.ShapeDtypeStruct((2, TOK, KVW), F32),
        ),
        in_specs=[smem_spec] * 3 + [vmem_spec, any_spec, any_spec, vmem_spec, vmem_spec, vmem_spec, any_spec],
        out_specs=(vmem_spec, vmem_spec, any_spec, vmem_spec, any_spec, vmem_spec, vmem_spec),
        scratch_shapes=[
            pltpu.VMEM((2, TOK, D), BF16),
            pltpu.VMEM((4 * ITEMS, 256, CHUNK), BF16),
            pltpu.VMEM((RANKS, 2, KVW, KVW), BF16),
            pltpu.VMEM((RANKS, 2, KVW, KVW), BF16),
            pltpu.VMEM((RANKS, TOK, KVW), BF16),
            pltpu.VMEM((RANKS, TOK, KVW), BF16),
            pltpu.VMEM((RANKS, 2 * TOK, KVW), BF16),
            pltpu.VMEM((2 * RANKS, HALF, DH), BF16),
            pltpu.VMEM((2 * RANKS, HALF, KVW), BF16),
            pltpu.VMEM((ITEMS, KVW, CHUNK), F32),
            pltpu.VMEM((2, ROWS, DH), BF16),
            pltpu.VMEM((2, DH, ROWS), BF16),
            pltpu.VMEM((2, ROWS, KVW), BF16),
            pltpu.VMEM((2, DH, ROWS), BF16),
            pltpu.VMEM((2, ROWS, KVW), F32),
            pltpu.VMEM((2, ROWS, DH), F32),
            pltpu.VMEM((2 * TOK, KVW), F32),
            pltpu.VMEM((2, TOK, KVW), F32),
            pltpu.VMEM((2 * TOK, KVW), BF16),
            pltpu.VMEM((KVW, 2 * TOK), BF16),
            dma((10,)),
            dma((320,)),
            dma((32,)),
            dma((32,)),
            dma((32,)),
            dma((32,)),
            dma((32,)),
            dma((32,)),
            dma((31,)),
            dma((31,)),
            dma,
            dma,
            dma((3,)),
            dma((3,)),
        ],
        compiler_params=pltpu.CompilerParams(
            collective_id=0, has_side_effects=True, vmem_limit_bytes=64 * MIB
        ),
        cost_estimate=pl.CostEstimate(
            flops=14 * 10**9, bytes_accessed=30 * MIB, transcendentals=TOK * HQ * SEQ
        ),
    )(table, rank_of_pair, pair_of_rank, gain, ahead, behind, ahead_queries, behind_queries, cotangent, weight)


BLOCKS = 4


def stream_kernel(own_ref, hidden_ref, weight_ref, gain_ref, grads_ref, stat_ref, out_ref):
    grads = grads_ref[...]
    inverse = stat_ref[0]
    inner = jnp.sum(grads.astype(F32) * stat_ref[1], axis=1, keepdims=True) * (1.0 / D)
    share = inverse * inverse * inner
    for k in range(BLOCKS):
        columns = slice(k * KVW, (k + 1) * KVW)
        grown = dot_t(grads, weight_ref[columns, :]) * gain_ref[:, columns]
        later = inverse * grown - hidden_ref[:, columns].astype(F32) * share
        later = later.astype(BF16).astype(F32)
        out_ref[:, columns] = (own_ref[:, columns].astype(F32) + later).astype(BF16)


def stream_call(own, hidden, weight, gain, grads, stats):
    wide = BLOCKS * KVW
    column_spec = pl.BlockSpec((TOK, wide), lambda i: (0, i))
    return pl.pallas_call(
        stream_kernel,
        name="stream",
        grid=(D // wide,),
        out_shape=jax.ShapeDtypeStruct((TOK, D), BF16),
        in_specs=[
            column_spec,
            column_spec,
            pl.BlockSpec((wide, KVW), lambda i: (i, 0)),
            pl.BlockSpec((1, wide), lambda i: (0, i)),
            pl.BlockSpec((TOK, KVW), lambda i: (0, 0)),
            pl.BlockSpec((2, TOK, KVW), lambda i: (0, 0, 0)),
        ],
        out_specs=column_spec,
        compiler_params=pltpu.CompilerParams(vmem_limit_bytes=40 * MIB),
        cost_estimate=pl.CostEstimate(
            flops=2 * TOK * D * KVW, bytes_accessed=20 * MIB, transcendentals=0
        ),
    )(own, hidden, weight, gain, grads, stats)


def body(
    ahead_hidden,
    ahead_queries,
    behind_hidden,
    behind_queries,
    behind_cotangent,
    keyval_weight,
    norm_gain,
    pair_of_rank,
):
    ctx_index = lax.axis_index("ctx").astype(jnp.int32)
    ranks = jnp.arange(RANKS, dtype=jnp.int32)
    rank_of_pair = jnp.sum(jnp.where(pair_of_rank[None, :] == ranks[:, None], ranks[None, :], 0), axis=1)
    table = lax.dynamic_index_in_dim(jnp.asarray(item_tables()), pair_of_rank[ctx_index], 0, keepdims=False)
    later_hidden = lax.ppermute(behind_hidden[0, 0], "pipe", [(1, 0)])
    later_gain = lax.ppermute(norm_gain[0].reshape(TOK, DH), "pipe", [(1, 0)])
    attention_out, query_grad, own_term, weight_grad, later_weight, later_grads, later_stats = whole_call(
        table,
        rank_of_pair,
        pair_of_rank,
        norm_gain[0].astype(F32).reshape(D // KVW, 1, KVW),
        ahead_hidden[0, 0],
        behind_hidden[0, 0],
        ahead_queries[0, 0],
        behind_queries[0, 0],
        behind_cotangent[0, 0],
        keyval_weight[0],
    )
    stream = stream_call(
        own_term,
        later_hidden,
        later_weight.reshape(D, KVW),
        later_gain.astype(F32).reshape(1, D),
        later_grads,
        later_stats,
    )
    return (
        attention_out[None, None],
        query_grad[None, None],
        stream[None, None],
        weight_grad[None],
    )


def solution(mesh):
    in_specs = (
        P("pipe", "dp", "ctx", None),
        P("pipe", "dp", "ctx", None),
        P("pipe", "dp", "ctx", None),
        P("pipe", "dp", "ctx", None),
        P("pipe", "dp", "ctx", None),
        P("pipe", ("ctx", "dp"), None),
        P("pipe", None),
        P(),
    )
    out_specs = (
        P("pipe", "dp", "ctx", None),
        P("pipe", "dp", "ctx", None),
        P("pipe", "dp", "ctx", None),
        P("pipe", ("ctx", "dp"), None),
    )
    return jax.shard_map(body, mesh=mesh, in_specs=in_specs, out_specs=out_specs, check_vma=False)
```

time: 317 us -> 290 us (0.915)
  Pallas kernels: 277 us -> 263 us
  between operations: 14.2 us -> 2.62 us
  starting transfers between devices: 12.1 us -> 5.77 us
  waiting for transfers between devices: 4.74 us -> 0.01 us
  local copies, waits for them, and re-layouts: 4.46 us -> 8.72 us
  other arithmetic: 1.05 us -> 5.22 us
    pallas_call x3 -> x1, Pallas kernels: 259 us -> 248 us  [whole_call(): pl.pallas_call(whole_kernel, name='layer_window', out_shape=(jax.ShapeDty...]
    ppermute x5 -> x2, starting transfers between devices: 12 us -> 5.77 us  [the longest x1 3.89 us: body(): later_hidden = lax.ppermute(behind_hidden[0, 0], 'pipe', [(1, 0)])]
    ppermute x5 -> x2, waiting for transfers between devices: 4.7 us -> 0.01 us  [the longest x1 0.01 us: body(): later_gain = lax.ppermute(norm_gain[0].reshape(TOK, DH), 'pipe', [(1, 0)])]
  transfers between devices with their start and end apart: 6 -> 2, of which waited for: 2 -> 0; matrix products, arithmetic and copies ran while one was open for 0% -> 3% of each run, Pallas kernels for 83% -> 87%
where the time goes in v2:
time: 290 us; the launch traced here: 285 us
  Pallas kernels  263 us (91%)
  local copies, waits for them, and re-layouts  8.72 us (3%)
  starting transfers between devices  5.77 us (2%)
  other arithmetic  5.22 us (2%)
    pallas_call x1, Pallas kernels, whole_call(): pl.pallas_call(whole_kernel, name='layer_window', out_shape=(jax.ShapeDty...  248 us
    pallas_call x1, Pallas kernels, stream_call(): pl.pallas_call(stream_kernel, name='stream', grid=(D // wide,), out_shape...  14.5 us
    unnamed x15, local copies, waits for them, and re-layouts  6.27 us
  transfers between devices with their start and end apart: 2, of which 0 were waited for; matrix products, arithmetic and copies ran while one was open for 3% of the time, Pallas kernels for 87%

profile of v2, /device:TPU:32, one launch (start us, length us, event | category | flops | bytes accessed | tf_op | source)
XLA Modules:
  0.0 285.0 jit_solution(12174811573250230091)
XLA Ops:
  0.6 3.9 %collective-permute-start = (bf16[128,16384]{1,0:T(8,128)(2,1)}, bf16[128,16384]{1,0:T(8,128)(2,1)}, u32[]{:S(2)}, u32[]{:S(2)}) collective-permute-start(bf16[128,16384]{1,0:T(8,128)(2,1)} %bitcast.26), channel_id=1, source_target_pairs={{64,0},{65,1},{66,2},{67,3},{68,4},{69,5},{70,6},{71,7},{72,8},{73... | collective-permute-start | bytes 12582920 | tf_op jit(solution)/shard_map/ppermute | solution.py:858
  4.5 1.6 reduce
  6.1 1.9 collective-permute-start.1
  8.0 1.2 dynamic_slice.7
  10.6 1.5 convert.2.gain_ref
  12.8 1.2 dynamic-slice_bitcast_fusion.table
  14.0 1.3 select_reduce_fusion.rank_of_pair
  15.2 248.2 %layer_window.1 = (bf16[128,2048]{1,0:T(8,128)(2,1)}, bf16[128,2048]{1,0:T(8,128)(2,1)}, bf16[128,16384]{1,0:T(8,128)(2,1)}, f32[256,256]{1,0:T(8,128)}, bf16[32...) custom-call(s32[64]{0:T(128)} %dynamic-slice_bitcast_fusion.table, ...), custom_call_target="tpu_custom_call" | custom-call | flops 14000000000 | bytes 31457280 | tf_op jit(solution)/shard_map/layer_window/pallas_call | solution.py:745
  263.4 0.0 collective-permute-done.1
  263.4 0.8 reshape.34
  264.2 0.0 collective-permute-done.hidden_ref
  264.2 0.0 copy-start
  264.2 2.2 copy-done
  266.4 0.0 copy-start.1
  266.4 0.9 copy-done.1
  267.3 0.0 copy-start.2
  267.3 0.8 copy-done.2
  268.2 0.0 copy-start.4
  268.2 0.0 copy-start.3
  268.2 0.0 copy-start.5
  268.2 14.5 %stream.1 = bf16[128,16384]{1,0:T(8,128)(2,1)} custom-call(bf16[128,16384]{1,0:T(8,128)(2,1)S(1)} %copy-done, bf16[128,16384]{1,0:T(8,128)(2,1)} %collective-permute-done.hidden_ref, bf16[16384,256]{1,0:T(8,128)(2,1)} %bitcast.19, f32[1,16384]{1,0:T(1,128)S(1)} %bitcast.18, bf16[128,256]{1,0:T(8,128)(2,1)S(1)} %copy-done.2, f32[2,128,256]{2,1,0:T(8,128)S(1)} %copy-done.1), custom_call_target="tpu_custom_call" | custom-call | flops 1073741824 | bytes 20971520 | tf_op jit(solution)/shard_map/stream/pallas_call | solution.py:823
  282.7 0.0 copy-done.4
  282.7 0.8 copy.16
  283.5 0.0 copy-done.3
  283.5 0.8 copy.17
  284.3 0.0 copy-done.5
  284.3 0.7 copy.18
Async XLA Ops:
  0.6 263.6 %collective-permute-start = (bf16[128,16384]{1,0:T(8,128)(2,1)}, bf16[128,16384]{1,0:T(8,128)(2,1)}, u32[]{:S(2)}, u32[]{:S(2)}) collective-permute-start(bf16[128,16384]{1,0:T(8,128)(2,1)} %bitcast.26), channel_id=1, source_target_pairs={{64,0},{65,1},{66,2},{67,3},{68,4},{69,5},{70,6},{71,7},{72,8},{73... | collective-permute-start | bytes 12582920 | tf_op jit(solution)/shard_map/ppermute | solution.py:858
  6.1 257.3 %collective-permute-start.1 = (bf16[128,128]{1,0:T(8,128)(2,1)}, bf16[128,128]{1,0:T(8,128)(2,1)}, u32[]{:S(2)}, u32[]{:S(2)}) collective-permute-start(bf16[128,128]{1,0:T(8,128)(2,1)} %bitcast.16), channel_id=1, source_target_pairs={{64,0},{65,1},{66,2},{67,3},{68,4},{69,5},{70,6},{71,7},{72,8},{73... | collective-permute-start | bytes 98312 | tf_op jit(solution)/shard_map/ppermute | solution.py:859
  264.2 2.2 copy-start
  266.4 0.9 copy-start.1
  267.3 0.8 copy-start.2
  268.2 14.5 %copy-start.4 = (bf16[128,2048]{1,0:T(8,128)(2,1)S(1)}, bf16[128,2048]{1,0:T(8,128)(2,1)}, u32[]{:S(2)}) copy-start(bf16[128,2048]{1,0:T(8,128)(2,1)} %get-tuple-element.11) | copy-start | bytes 1572868
  268.2 15.3 %copy-start.3 = (bf16[128,2048]{1,0:T(8,128)(2,1)S(1)}, bf16[128,2048]{1,0:T(8,128)(2,1)}, u32[]{:S(2)}) copy-start(bf16[128,2048]{1,0:T(8,128)(2,1)} %get-tuple-element.12) | copy-start | bytes 1572868
  268.2 16.1 %copy-start.5 = (f32[256,256]{1,0:T(8,128)S(1)}, f32[256,256]{1,0:T(8,128)}, u32[]{:S(2)}) copy-start(f32[256,256]{1,0:T(8,128)} %get-tuple-element.17) | copy-start | bytes 786436

commit v3 on v2

--- a/solution.py
+++ b/solution.py
@@ -59,6 +59,10 @@
     def section_mate(self):
         return (1 - self.pipe, self.ctx, self.core)
 
+    def section_diagonal(self):
+
+        return (1 - self.pipe, self.slot(0, 0, 1), self.core)
+
     def barrier(self):
         semaphore = pltpu.get_barrier_semaphore()
         partners = [
@@ -69,6 +73,7 @@
             self.device(0, -1, 0),
             self.sibling(),
             self.section_mate(),
+            self.section_diagonal(),
         ]
         for partner in partners:
             pl.semaphore_signal(semaphore, inc=1, device_id=partner, device_id_type=MESH)
@@ -282,8 +287,8 @@
 
 
 class Attention:
-    def __init__(self, table, rank_of_pair, keys, values, rows, weights, summed):
-        self.table, self.rank_of_pair = table, rank_of_pair
+    def __init__(self, table, keys, values, rows, weights, summed):
+        self.table = table
         self.keys, self.values, self.rows = keys, values, rows
         self.weights, self.summed = weights, summed
 
@@ -292,7 +297,7 @@
 
         @pl.loop(0, RANKS)
         def _(b):
-            rank = self.rank_of_pair[b]
+            rank = self.table[64 + b]
             for part, block in ((0, b), (1, 2 * RANKS - 1 - b)):
                 source = keyval[rank, part * HALF : (part + 1) * HALF, :]
                 self.keys[block] = source[:, :DH]
@@ -343,7 +348,6 @@
 
 def whole_kernel(
     table,
-    rank_of_pair,
     pair_of_rank,
     gain_ref,
     ahead_ref,
@@ -357,8 +361,9 @@
     own_term_out,
     weight_grad_out,
     later_weights_out,
+    later_gain_out,
     later_grads_out,
-    later_stats_out,
+    later_rows_out,
     hidden,
     big,
     weights,
@@ -376,7 +381,9 @@
     summed,
     grad_rows,
     total,
-    stats,
+    gain,
+    gain_lines,
+    row_terms,
     both,
     both_t,
     load_sems,
@@ -408,23 +415,36 @@
 
     is_later = place.pipe == 1
     is_earlier = place.pipe == 0
-    crossing = [
-        (weight_ref, later_weights.at[ctx, core]),
-        (stats, later_stats_out),
-        (both.at[pl.ds(pl.multiple_of(core * TOK, TOK), TOK)], later_grads_out),
-    ]
-    crossings = [
-        pltpu.make_async_remote_copy(
+    def mirror(slot):
+        return slot + 4 - 8 * ((slot // 4) % 2)
+
+    def crossing(k, src, dst, device):
+        return pltpu.make_async_remote_copy(
             src_ref=src,
             dst_ref=dst,
             send_sem=section_send.at[k],
             recv_sem=section_recv.at[k],
-            device_id=place.section_mate(),
+            device_id=device,
             device_id_type=MESH,
         )
-        for k, (src, dst) in enumerate(crossing)
+
+    mine = pl.ds(pl.multiple_of(core * TOK, TOK), TOK)
+    theirs = pl.ds(pl.multiple_of((1 - core) * TOK, TOK), TOK)
+    mate = place.section_mate()
+    first_crossing = crossing(0, weight_ref, later_weights.at[ctx, core], place.section_diagonal())
+    last_crossings = [
+        crossing(1, gain_lines, later_gain_out, mate),
+        crossing(2, row_terms, later_rows_out, mate),
+        crossing(3, both.at[mine], later_grads_out, mate),
     ]
-    own_later = pltpu.make_async_copy(weight_ref, later_weights.at[ctx, core], load_sems.at[4])
+    own_later = pltpu.make_async_copy(
+        weight_ref, later_weights.at[mirror(ctx), core], load_sems.at[4]
+    )
+    for j in range(D // KVW):
+        gain[j] = gain_ref[:, j * KVW : (j + 1) * KVW].astype(F32)
+        for k in range(2):
+            columns = slice((2 * j + k) * DH, (2 * j + k + 1) * DH)
+            gain_lines[2 * j + k : 2 * j + k + 1, :] = gain_ref[:, columns].astype(F32)
 
     place.barrier()
     loads[2].wait()
@@ -432,8 +452,9 @@
     @pl.when(is_later)
     def _():
         own_later.start()
-        crossings[0].start()
-        later_stats_out[...] = jnp.zeros_like(later_stats_out)
+        first_crossing.start()
+        later_gain_out[...] = jnp.zeros_like(later_gain_out)
+        later_rows_out[...] = jnp.zeros_like(later_rows_out)
         later_grads_out[...] = jnp.zeros_like(later_grads_out)
 
     total[...] = jnp.zeros_like(total)
@@ -452,11 +473,11 @@
     def scale_rows(batch, part):
         inverse = inverses[batch]
 
-        @pl.loop(part * 16, part * 16 + 16)
+        @pl.loop(part * 8, part * 8 + 8)
         def _(i):
             for k in range(2):
                 columns = pl.ds(pl.multiple_of((2 * i + k) * KVW, KVW), KVW)
-                block = hidden[batch, :, columns].astype(F32) * inverse * gain_ref[2 * i + k]
+                block = hidden[batch, :, columns].astype(F32) * inverse * gain[2 * i + k]
                 big[i, batch * TOK : (batch + 1) * TOK, k * KVW : (k + 1) * KVW] = block.astype(BF16)
 
     def term_got(k):
@@ -465,8 +486,6 @@
     def half(which):
         return pl.ds(pl.multiple_of(which * KVW, KVW), KVW)
 
-    mine = pl.ds(pl.multiple_of(core * TOK, TOK), TOK)
-    theirs = pl.ds(pl.multiple_of((1 - core) * TOK, TOK), TOK)
     own_pair = pltpu.make_async_copy(
         big.at[pl.ds(0, RANKS), pl.ds(TOK, TOK), half(core)], pairs.at[:, mine, :], load_sems.at[3]
     )
@@ -484,9 +503,13 @@
         lambda: (loads[0].wait(), row_scale(1)),
         lambda: scale_rows(1, 0),
         lambda: scale_rows(1, 1),
-        lambda: (send_pair(), loads[1].wait(), row_scale(0)),
+        lambda: scale_rows(1, 2),
+        lambda: (scale_rows(1, 3), send_pair()),
+        lambda: (loads[1].wait(), row_scale(0)),
         lambda: scale_rows(0, 0),
         lambda: scale_rows(0, 1),
+        lambda: scale_rows(0, 2),
+        lambda: scale_rows(0, 3),
     ]
     ready = []
     taken = [0]
@@ -501,9 +524,9 @@
         sender.landed(weights.at[slot, 1 - core], sibling_recv.at[rid(du, dv, zr)], place.sibling())
         project(slot, 1 - core)
 
-    def relay_to_sibling(buffer, recv):
+    def relay_to_sibling(buffer, recv, where):
         def send(slot, du, dv, zr):
-            here = buffer.at[slot, core]
+            here = buffer.at[where(slot), core]
             sender.push(here, here, recv.at[rid(du, dv, zr)], place.sibling())
 
         return send
@@ -513,25 +536,28 @@
         sender,
         lambda slot: weights.at[slot, core],
         weight_recv,
-        relay_to_sibling(weights, sibling_recv),
+        relay_to_sibling(weights, sibling_recv, lambda slot: slot),
     )
     for arrived, slot in enumerate(first):
         ready.append(slot)
+        if arrived < 6:
+            continue
         if todo:
             todo.pop(0)()
             continue
-        while ready:
-            project(ready.pop(0), core)
-        for _ in range(2):
+        for _ in range(3):
+            if ready:
+                project(ready.pop(0), core)
             if taken[0] < arrived - 1:
                 take_sibling()
+    while ready:
+        project(ready.pop(0), core)
     while taken[0] < len(SIBLING_ORDER):
         take_sibling()
 
     keyvals[ctx] = total[TOK:, :].astype(BF16)
     ahead_keyvals[ctx] = total[:TOK, :].astype(BF16)
-    stats[0] = jnp.broadcast_to(inverses[1], (TOK, KVW))
-    stats[1] = total[TOK:, :]
+    row_terms[:, :DH] = jnp.broadcast_to(inverses[1], (TOK, DH))
 
     def prepare(part):
         rows[part] = stack(behind_queries, part)
@@ -549,12 +575,11 @@
 
     @pl.when(is_later)
     def _():
-        crossings[1].start()
         own_later.wait()
 
     @pl.when(is_earlier)
     def _():
-        crossings[0].wait_recv()
+        sender.landed(later_weights.at[mirror(ctx), core], section_recv.at[0], mate)
 
     ahead_sender = Sender(send_sems, 256)
     ahead = ring_gather(
@@ -563,9 +588,9 @@
     later = ring_gather(
         place,
         sender,
-        lambda slot: later_weights.at[slot, core],
+        lambda slot: later_weights.at[mirror(slot), core],
         later_recv,
-        relay_to_sibling(later_weights, later_sibling_recv),
+        relay_to_sibling(later_weights, later_sibling_recv, mirror),
     )
 
     def serve(gathers):
@@ -573,14 +598,15 @@
             next(gather, None)
 
     serve((ahead, later))
-    attention = Attention(table, rank_of_pair, keys, values, rows, big, summed)
+    attention = Attention(table, keys, values, rows, big, summed)
     attention.order(keyvals)
     for copy in sender.copies[:second_sends]:
         copy.wait_send()
     own_pair.wait()
     for i in range(ITEMS):
         attention.weigh(i, True)
-        serve((ahead, later))
+        if i % 3 == 2:
+            serve((ahead, later))
     for part in range(2):
         cotangent = stack(cotangent_ref, part).astype(F32)
         inverse = 1.0 / summed[part, :, DH:]
@@ -640,13 +666,18 @@
         if todo:
             todo.pop(0)()
         serve((ahead, later))
+        serve((ahead, later))
     key_grads = result[0].astype(BF16)
     both[mine, :] = key_grads
     sender.push(both.at[mine], both.at[mine], both_recv, place.sibling())
+    inverse = row_terms[:, :DH]
+    inner = jnp.sum(key_grads.astype(F32) * total[TOK:, :], axis=1, keepdims=True) * (1.0 / D)
+    row_terms[:, DH:] = inverse * inverse * inner
 
     @pl.when(is_later)
     def _():
-        crossings[2].start()
+        for last_crossing in last_crossings:
+            last_crossing.start()
 
     for _ in ahead:
         serve((later,))
@@ -671,9 +702,8 @@
         make,
         result,
     )
-    inner = jnp.sum(key_grads.astype(F32) * stats[1], axis=1, keepdims=True) * (1.0 / D)
-    inverse = stats[0]
-    share = inverse * inverse * inner
+    inverse = row_terms[:, :1]
+    share = row_terms[:, DH : DH + 1]
 
     store_later = pltpu.make_async_copy(later_weights, later_weights_out, load_sems.at[5])
     todo = [lambda k=k: [attention.weigh(i, False) for i in range(3 * k, 3 * k + 3)] for k in range(3)]
@@ -688,7 +718,7 @@
         for du, dv, zr in SIBLING_ORDER:
             slot = place.sibling_slot(du, dv, zr)
             sender.landed(
-                later_weights.at[slot, 1 - core], later_sibling_recv.at[rid(du, dv, zr)], place.sibling()
+                later_weights.at[mirror(slot), 1 - core], later_sibling_recv.at[rid(du, dv, zr)], place.sibling()
             )
 
         store_later.start()
@@ -701,7 +731,7 @@
         def _(slot):
             for k in range(2):
                 columns = pl.ds(pl.multiple_of((2 * slot + k) * KVW, KVW), KVW)
-                grown = dot_t(key_grads, weights[slot, k]) * gain_ref[2 * slot + k]
+                grown = dot_t(key_grads, weights[slot, k]) * gain[2 * slot + k]
                 own = inverse * grown - hidden[1, :, columns].astype(F32) * share
                 hidden[1, :, columns] = own.astype(BF16)
 
@@ -728,16 +758,17 @@
 
     @pl.when(is_later)
     def _():
-        for crossing_copy in crossings:
-            crossing_copy.wait_send()
+        first_crossing.wait_send()
+        for last_crossing in last_crossings:
+            last_crossing.wait_send()
 
     @pl.when(is_earlier)
     def _():
-        for crossing_copy in crossings[1:]:
-            crossing_copy.wait_recv()
-
-
-def whole_call(table, rank_of_pair, pair_of_rank, gain, ahead, behind, ahead_queries, behind_queries, cotangent, weight):
+        for last_crossing in last_crossings:
+            last_crossing.wait_recv()
+
+
+def whole_call(table, pair_of_rank, gain, ahead, behind, ahead_queries, behind_queries, cotangent, weight):
     any_spec = pl.BlockSpec(memory_space=pl.ANY)
     vmem_spec = pl.BlockSpec(memory_space=pltpu.VMEM)
     smem_spec = pl.BlockSpec(memory_space=pltpu.SMEM)
@@ -751,11 +782,12 @@
             jax.ShapeDtypeStruct((TOK, D), BF16),
             jax.ShapeDtypeStruct((KVW, KVW), F32),
             jax.ShapeDtypeStruct((RANKS, 2, KVW, KVW), BF16),
+            jax.ShapeDtypeStruct((D // DH, DH), F32),
             jax.ShapeDtypeStruct((TOK, KVW), BF16),
-            jax.ShapeDtypeStruct((2, TOK, KVW), F32),
+            jax.ShapeDtypeStruct((TOK, KVW), F32),
         ),
-        in_specs=[smem_spec] * 3 + [vmem_spec, any_spec, any_spec, vmem_spec, vmem_spec, vmem_spec, any_spec],
-        out_specs=(vmem_spec, vmem_spec, any_spec, vmem_spec, any_spec, vmem_spec, vmem_spec),
+        in_specs=[smem_spec] * 2 + [vmem_spec, any_spec, any_spec, vmem_spec, vmem_spec, vmem_spec, any_spec],
+        out_specs=(vmem_spec, vmem_spec, any_spec, vmem_spec, any_spec, vmem_spec, vmem_spec, vmem_spec),
         scratch_shapes=[
             pltpu.VMEM((2, TOK, D), BF16),
             pltpu.VMEM((4 * ITEMS, 256, CHUNK), BF16),
@@ -774,7 +806,9 @@
             pltpu.VMEM((2, ROWS, KVW), F32),
             pltpu.VMEM((2, ROWS, DH), F32),
             pltpu.VMEM((2 * TOK, KVW), F32),
-            pltpu.VMEM((2, TOK, KVW), F32),
+            pltpu.VMEM((D // KVW, 1, KVW), F32),
+            pltpu.VMEM((D // DH, DH), F32),
+            pltpu.VMEM((TOK, KVW), F32),
             pltpu.VMEM((2 * TOK, KVW), BF16),
             pltpu.VMEM((KVW, 2 * TOK), BF16),
             dma((10,)),
@@ -789,8 +823,8 @@
             dma((31,)),
             dma,
             dma,
-            dma((3,)),
-            dma((3,)),
+            dma((4,)),
+            dma((4,)),
         ],
         compiler_params=pltpu.CompilerParams(
             collective_id=0, has_side_effects=True, vmem_limit_bytes=64 * MIB
@@ -798,28 +832,28 @@
         cost_estimate=pl.CostEstimate(
             flops=14 * 10**9, bytes_accessed=30 * MIB, transcendentals=TOK * HQ * SEQ
         ),
-    )(table, rank_of_pair, pair_of_rank, gain, ahead, behind, ahead_queries, behind_queries, cotangent, weight)
-
-
-BLOCKS = 4
-
-
-def stream_kernel(own_ref, hidden_ref, weight_ref, gain_ref, grads_ref, stat_ref, out_ref):
+    )(table, pair_of_rank, gain, ahead, behind, ahead_queries, behind_queries, cotangent, weight)
+
+
+BLOCKS = 8
+
+
+def stream_kernel(own_ref, hidden_ref, weight_ref, gain_ref, grads_ref, rows_ref, out_ref):
     grads = grads_ref[...]
-    inverse = stat_ref[0]
-    inner = jnp.sum(grads.astype(F32) * stat_ref[1], axis=1, keepdims=True) * (1.0 / D)
-    share = inverse * inverse * inner
+    inverse = rows_ref[:, :1]
+    share = rows_ref[:, DH : DH + 1]
     for k in range(BLOCKS):
         columns = slice(k * KVW, (k + 1) * KVW)
-        grown = dot_t(grads, weight_ref[columns, :]) * gain_ref[:, columns]
+        grown = dot_t(grads, weight_ref[columns, :]) * jnp.concatenate([gain_ref[2 * k : 2 * k + 1, :], gain_ref[2 * k + 1 : 2 * k + 2, :]], axis=1)
         later = inverse * grown - hidden_ref[:, columns].astype(F32) * share
         later = later.astype(BF16).astype(F32)
         out_ref[:, columns] = (own_ref[:, columns].astype(F32) + later).astype(BF16)
 
 
-def stream_call(own, hidden, weight, gain, grads, stats):
+def stream_call(own, hidden, weight, gain, grads, rows):
     wide = BLOCKS * KVW
     column_spec = pl.BlockSpec((TOK, wide), lambda i: (0, i))
+    later_spec = pl.BlockSpec((TOK, wide), lambda i: (1, i))
     return pl.pallas_call(
         stream_kernel,
         name="stream",
@@ -827,18 +861,18 @@
         out_shape=jax.ShapeDtypeStruct((TOK, D), BF16),
         in_specs=[
             column_spec,
-            column_spec,
+            later_spec,
             pl.BlockSpec((wide, KVW), lambda i: (i, 0)),
-            pl.BlockSpec((1, wide), lambda i: (0, i)),
+            pl.BlockSpec((2 * BLOCKS, DH), lambda i: (i, 0)),
             pl.BlockSpec((TOK, KVW), lambda i: (0, 0)),
-            pl.BlockSpec((2, TOK, KVW), lambda i: (0, 0, 0)),
+            pl.BlockSpec((TOK, KVW), lambda i: (0, 0)),
         ],
         out_specs=column_spec,
-        compiler_params=pltpu.CompilerParams(vmem_limit_bytes=40 * MIB),
+        compiler_params=pltpu.CompilerParams(vmem_limit_bytes=62 * MIB),
         cost_estimate=pl.CostEstimate(
             flops=2 * TOK * D * KVW, bytes_accessed=20 * MIB, transcendentals=0
         ),
-    )(own, hidden, weight, gain, grads, stats)
+    )(own, hidden, weight, gain, grads, rows)
 
 
 def body(
@@ -852,16 +886,19 @@
     pair_of_rank,
 ):
     ctx_index = lax.axis_index("ctx").astype(jnp.int32)
-    ranks = jnp.arange(RANKS, dtype=jnp.int32)
-    rank_of_pair = jnp.sum(jnp.where(pair_of_rank[None, :] == ranks[:, None], ranks[None, :], 0), axis=1)
-    table = lax.dynamic_index_in_dim(jnp.asarray(item_tables()), pair_of_rank[ctx_index], 0, keepdims=False)
-    later_hidden = lax.ppermute(behind_hidden[0, 0], "pipe", [(1, 0)])
-    later_gain = lax.ppermute(norm_gain[0].reshape(TOK, DH), "pipe", [(1, 0)])
-    attention_out, query_grad, own_term, weight_grad, later_weight, later_grads, later_stats = whole_call(
+    ranks = np.arange(RANKS, dtype=np.int32)
+    holds = (pair_of_rank[:, None] == ranks[None, :])[None]
+    lines = jnp.asarray(item_tables().T)
+    of_own = jnp.where(ranks[None, :, None] == ctx_index, lines[:, None, :], 0)
+    of_pair = jnp.asarray(
+        np.broadcast_to(ranks[None, :, None] * (ranks[:, None, None] == ranks[None, None, :]), (RANKS,) * 3)
+    )
+    table = jnp.sum(jnp.where(holds, jnp.concatenate([of_own, of_pair]), 0), axis=(1, 2))
+    later_hidden = lax.all_gather(behind_hidden[0, 0], "pipe", axis=0, tiled=True)
+    outs = whole_call(
         table,
-        rank_of_pair,
         pair_of_rank,
-        norm_gain[0].astype(F32).reshape(D // KVW, 1, KVW),
+        norm_gain,
         ahead_hidden[0, 0],
         behind_hidden[0, 0],
         ahead_queries[0, 0],
@@ -869,13 +906,14 @@
         behind_cotangent[0, 0],
         keyval_weight[0],
     )
+    attention_out, query_grad, own_term, weight_grad, later_weight, later_gain, later_grads, later_rows = outs
     stream = stream_call(
         own_term,
         later_hidden,
         later_weight.reshape(D, KVW),
-        later_gain.astype(F32).reshape(1, D),
+        later_gain,
         later_grads,
-        later_stats,
+        later_rows,
     )
     return (
         attention_out[None, None],

time: 290 us -> 199 us (0.69); the launches traced: 285 us -> 200 us
  Pallas kernels: 263 us -> 181 us
  between operations: 2.62 us -> 14.3 us
  local copies, waits for them, and re-layouts: 8.72 us -> 2.41 us
  starting transfers between devices: 5.77 us -> 0.04 us
  other arithmetic: 5.22 us -> 1.06 us
    pallas_call x1, Pallas kernels: 248 us -> 170 us  [whole_call(): pl.pallas_call(whole_kernel, name='layer_window', out_shape=(jax.ShapeDty...]
    ppermute x2 -> x0, starting transfers between devices: 5.77 us -> none  [the longest x1 3.89 us: body(): later_hidden = lax.ppermute(behind_hidden[0, 0], 'pipe', [(1, 0)])]
    unnamed x15 -> x17, local copies, waits for them, and re-layouts: 6.27 us -> 2.41 us
    pallas_call x1, Pallas kernels: 14.5 us -> 11.4 us  [stream_call(): pl.pallas_call(stream_kernel, name='stream', grid=(D // wide,), out_shape...]
  transfers between devices with their start and end apart: 2 -> 1, of which waited for: 0 -> 0; matrix products, arithmetic and copies ran while one was open for 3% -> 1% of each run, Pallas kernels for 87% -> 85%
where the time goes in v3:
time: 199 us; the launch traced here: 200 us
  Pallas kernels  181 us (91%)
  between operations  14.3 us (7%)
  local copies, waits for them, and re-layouts  2.41 us (1%)
    pallas_call x1, Pallas kernels, whole_call(): pl.pallas_call(whole_kernel, name='layer_window', out_shape=(jax.ShapeDty...  170 us
    pallas_call x1, Pallas kernels, stream_call(): pl.pallas_call(stream_kernel, name='stream', grid=(D // wide,), out_shape...  11.4 us
  transfers between devices with their start and end apart: 1, of which 0 were waited for; matrix products, arithmetic and copies ran while one was open for 1% of the time, Pallas kernels for 85%

profile of v3, /device:TPU:32, one launch (start us, length us, event | category | flops | bytes accessed | tf_op | source)
XLA Modules:
  0.0 199.9 jit_solution(11173992248192691983)
XLA Ops:
  7.2 0.0 copy-start.6
  7.2 0.0 copy-start.4
  7.2 0.0 copy-start.2
  7.2 0.0 copy-start.5
  7.2 0.0 all-gather.3.cloned.1.call-start
  7.3 0.7 all-gather.3.cloned.1.call-update
  8.0 0.0 copy-done.6
  8.0 0.0 copy-done.5
  8.0 0.1 iota_compare_fusion
  8.1 0.0 copy-done.4
  8.1 0.1 broadcast_select_fusion
  8.2 0.1 copy-done.2
  8.3 0.9 fusion.table
  9.1 170.0 %layer_window.1 = (bf16[128,2048]{1,0:T(8,128)(2,1)}, bf16[128,2048]{1,0:T(8,128)(2,1)}, bf16[128,16384]{1,0:T(8,128)(2,1)}, f32[256,256]{1,0:T(8,128)}, bf16[32...) custom-call(s32[96]{0:T(128)} %fusion.table, s32[32]{0:T(128)} %pair_of_rank.1, ...), custom_call_target="tpu_custom_call" | custom-call | flops 14000000000 | bytes 31457280 | tf_op jit(solution)/shard_map/layer_window/pallas_call | solution.py:776
  179.1 0.0 all-gather.3.cloned.1.call-done
  179.1 0.0 copy-start.1
  179.2 0.0 copy-start
  179.2 0.0 copy-start.3
  179.2 11.4 %stream.1 = bf16[128,16384]{1,0:T(8,128)(2,1)} custom-call(bf16[128,16384]{1,0:T(8,128)(2,1)} %get-tuple-element.14.own_ref, bf16[256,16384]{1,0:T(8,128)(2,1)} %bitcast.14, bf16[16384,256]{1,0:T(8,128)(2,1)} %bitcast.15, f32[128,128]{1,0:T(8,128)} %get-tuple-element.16.gain_ref, bf16[128,256]{1,0:T(8,128)(2,1)} %get-tuple-element.17.grads_ref, ...), custom_call_target="tpu_custom_call" | custom-call | flops 1073741824 | bytes 20971520 | tf_op jit(solution)/shard_map/stream/pallas_call | solution.py:857
  190.6 0.0 copy-done.1
  190.6 0.8 copy.19
  191.4 0.0 copy-done
  191.4 0.8 copy.20
  192.2 0.0 copy-done.3
  192.2 0.7 copy.21
  (1 shorter events, 0.0 us)
Async XLA Ops:
  7.2 0.8 copy-start.6
  7.2 0.9 copy-start.4
  7.2 1.1 copy-start.2
  7.2 0.8 copy-start.5
  7.2 171.9 %all-gather.3.cloned.1.call-start = ((), (), s32[]{:S(2)}) async-start(), calls=%async_computation | async-start | bytes 12582912 | tf_op jit(solution)/shard_map/all_gather | solution.py:897
  179.1 11.5 %copy-start.1 = (bf16[128,2048]{1,0:T(8,128)(2,1)S(1)}, bf16[128,2048]{1,0:T(8,128)(2,1)}, u32[]{:S(2)}) copy-start(bf16[128,2048]{1,0:T(8,128)(2,1)} %get-tuple-element.12) | copy-start | bytes 1572868
  179.2 12.3 %copy-start = (bf16[128,2048]{1,0:T(8,128)(2,1)S(1)}, bf16[128,2048]{1,0:T(8,128)(2,1)}, u32[]{:S(2)}) copy-start(bf16[128,2048]{1,0:T(8,128)(2,1)} %get-tuple-element.13) | copy-start | bytes 1572868
  179.2 13.0 %copy-start.3 = (f32[256,256]{1,0:T(8,128)S(1)}, f32[256,256]{1,0:T(8,128)}, u32[]{:S(2)}) copy-start(f32[256,256]{1,0:T(8,128)} %get-tuple-element.19) | copy-start | bytes 786436
Sparse Core Ops, SparseCore 0:
  9.7 112.9 all-gather.2
